TPU v7x, 128 devices: a whole 4x4x4 slice. The times are simulated.
128 devices in a mesh: expert: 32 (over y, z, core), tensor: 4 (over x).
Axes of the slice: x: 4, y: 4, z: 4, core: 2. Of those that a mesh axis runs over, the one named last changes fastest.
Arguments:
- tokens: bfloat16 [1024, 7168], P('expert'), may hold values from -6 to 6
- cotangent: bfloat16 [1024, 7168], P('expert'), may hold values from -1.5 to 1.5
- gate_weights: bfloat16 [1024, 8], P('expert'), may hold values from 0.019897461 to 0.5
- route_slots: int32 [1024, 8], P('expert'), may hold values from 0 to 31, all different within a row; in each aligned block of 32 rows (0 to 31, 32 to 63, ...) at most 12 rows name the same one
- replica_owner: int32 [4], replicated, may hold values from 0 to 27, as said below
- w_gate: bfloat16 [32, 7168, 1024], P('expert', None, 'tensor'), as said below
- w_up: bfloat16 [32, 7168, 1024], P('expert', None, 'tensor'), as said below
- w_down: bfloat16 [32, 7168, 1024], P('expert', None, 'tensor'), as said below
Outputs:
- input_grads: bfloat16 [1024, 7168], P('expert', 'tensor')
- gate_grads: bfloat16 [1024, 8], P('expert')
- expert_grads: bfloat16 [28, 7168, 3, 1024], P(None, 'expert', None, 'tensor')
Inputs may be any that keep to these rules, and one draw needn't show every extreme that they name: `route_slots`: in each block of 32 tokens no slot is named by more than 12 entries, a bound that some block reaches; a token names 8 different slots. `replica_owner`: numbers of experts; one expert may own several replicas, and a replica slot's weights equal its expert's. `w_gate`: slot 28 + r holds the same matrix as slot replica_owner[r]. `w_up`: slot 28 + r holds the same matrix as slot replica_owner[r]. `w_down`: slot 28 + r holds the same matrix as slot replica_owner[r].
All inputs are finite; a program needn't handle non-finite values.
Results may differ from a plain program's by a relative error of at most 0.012.
Values may be sent and summed in bfloat16 or wider, within the bound.
A program may use at most 128 MiB of HBM per device.

v0:
```python
import functools

import jax
import jax.numpy as jnp
from jax import lax
from jax.experimental import pallas as pl
from jax.experimental.pallas import tpu as pltpu
from jax.sharding import PartitionSpec as P

MESH = pl.DeviceIdType.MESH
BF = jnp.bfloat16
F32 = jnp.float32
LANE = 128
RING = 4
CORES = 2
MIB = 1 << 20
NT = (((1,), (1,)), ((), ()))
TN = (((0,), (0,)), ((), ()))


def dot(a, b, dims=None):
    if dims is None:
        return jnp.dot(a, b, preferred_element_type=F32)
    return lax.dot_general(a, b, dims, preferred_element_type=F32)


def up1(v):
    return lax.rem(v + 1, RING)


def down1(v):
    return lax.rem(v + RING - 1, RING)


def position():
    e = lax.axis_index("expert")
    t = lax.axis_index("tensor")
    return lax.div(e, CORES * RING), lax.rem(lax.div(e, CORES), RING), lax.rem(e, CORES), t


class Links:
    def __init__(self, send, recv):
        self.send, self.recv, self.count, self.started = send, recv, 0, []
        self.y, self.z, self.c, self.t = position()

    def to(self, y=None, z=None, c=None, t=None):
        y = self.y if y is None else y
        z = self.z if z is None else z
        c = self.c if c is None else c
        t = self.t if t is None else t
        return ((y * RING + z) * CORES + c, t)

    def start(self, src, dst, device):
        copy = pltpu.make_async_remote_copy(
            src_ref=src,
            dst_ref=dst,
            send_sem=self.send.at[self.count],
            recv_sem=self.recv.at[self.count],
            device_id=device,
            device_id_type=MESH,
        )
        self.count += 1
        copy.start()
        self.started.append(copy)
        return copy

    def greet(self, devices):
        barrier = pltpu.get_barrier_semaphore()
        for device in devices:
            pl.semaphore_signal(barrier, inc=1, device_id=device, device_id_type=MESH)
        pl.semaphore_wait(barrier, len(devices))

    def plane(self):
        return [
            self.to(y=up1(self.y)),
            self.to(y=down1(self.y)),
            self.to(z=up1(self.z)),
            self.to(z=down1(self.z)),
            self.to(c=1 - self.c),
        ]

    def drain(self):
        for copy in self.started:
            copy.wait_send()


class Gather:
    def __init__(self, links, at, y_first):
        self.l, self.at, self.y_first = links, at, y_first
        self.first = links.y if y_first else links.z
        self.second = links.z if y_first else links.y

    def place(self, first, second, part=None):
        return self.at(first, second, part) if self.y_first else self.at(second, first, part)

    def along_first(self, v):
        return self.l.to(y=v) if self.y_first else self.l.to(z=v)

    def along_second(self, v):
        return self.l.to(z=v) if self.y_first else self.l.to(y=v)

    def copy(self, ref, device):
        return self.l.start(ref, ref, device)

    def hand_over(self, second):
        ref = self.place(slice(None), second)
        return self.copy(ref, self.l.to(c=1 - self.l.c))

    def one(self):
        own = self.place(self.first, self.second)
        self.m1 = self.copy(own, self.along_first(up1(self.first)))
        self.m2 = self.copy(own, self.along_first(down1(self.first)))

    def two(self):
        self.m1.wait_recv()
        self.m3 = self.copy(
            self.place(down1(self.first), self.second, 0), self.along_first(up1(self.first))
        )
        self.m2.wait_recv()
        self.m4 = self.copy(
            self.place(up1(self.first), self.second, 1), self.along_first(down1(self.first))
        )

    def three(self):
        self.m3.wait_recv()
        self.m4.wait_recv()
        line = self.place(slice(None), self.second)
        self.m5 = self.copy(line, self.along_second(up1(self.second)))
        self.m6 = self.copy(line, self.along_second(down1(self.second)))
        self.s = [self.hand_over(self.second)]

    def four(self):
        low, high = down1(self.second), up1(self.second)
        self.m5.wait_recv()
        self.m7 = self.copy(self.place(slice(None), low, 0), self.along_second(high))
        self.s.append(self.hand_over(low))
        self.m6.wait_recv()
        self.m8 = self.copy(self.place(slice(None), high, 1), self.along_second(low))
        self.s.append(self.hand_over(high))

    def five(self):
        self.m7.wait_recv()
        self.m8.wait_recv()
        self.s.append(self.hand_over(up1(up1(self.second))))

    def six(self):
        for copy in self.s:
            copy.wait_recv()


GATHER_COPIES = 12


def entries(meta, slot, per, cap, top):
    count = meta.shape[0]
    pick = (
        lax.broadcasted_iota(jnp.int32, (2 * top, LANE), 0)
        == lax.broadcasted_iota(jnp.int32, (2 * top, LANE), 1)
    ).astype(F32).astype(BF)
    turned = dot(pick, meta, NT)
    slot = slot.astype(F32)
    hit = jnp.zeros((slot.shape[0], count), F32)
    gate = jnp.zeros((slot.shape[0], count), F32)
    for k in range(top):
        same = turned[k : k + 1] == slot
        hit = hit + jnp.where(same, 1.0, 0.0)
        gate = gate + jnp.where(same, turned[top + k : top + k + 1], 0.0)
    earlier = lax.broadcasted_iota(jnp.int32, (count, count), 0)
    token = lax.broadcasted_iota(jnp.int32, (count, count), 1)
    before = jnp.where(
        (earlier < token) & (lax.div(earlier, per) == lax.div(token, per)), 1.0, 0.0
    ).astype(BF)
    place = dot(hit.astype(BF), before)
    block = lax.div(lax.broadcasted_iota(jnp.int32, hit.shape, 1), per).astype(F32)
    row = jnp.where(hit > 0.5, block * cap + place, -1.0)
    return row, gate, turned


def picks(row, group_rows):
    lines = lax.broadcasted_iota(jnp.int32, (group_rows, row.shape[1]), 0).astype(F32)
    return jnp.where(row == lines, 1.0, 0.0)


def dispatch_kernel(
    dims,
    tokens, cotangent, meta, w_gate, w_up, w_down,
    acts, score, cuts, meta_all,
    buf, wg, wu, wd, rows_buf, gate_acc, up_acc, down_acc, select, gate_rows,
    send, recv, local,
):
    per, width, cap, top, ff = dims
    slots = RING * RING * CORES
    group_rows = cap * slots // RING
    line = per * slots // RING
    links = Links(send, recv)
    y, z, c = links.y, links.z, links.c
    me = lax.axis_index("expert")
    x0, dy0 = LANE, LANE + width
    end = LANE + 2 * width
    loads = [
        pltpu.make_async_copy(meta, buf.at[y, z, c, :, pl.ds(0, LANE)], local.at[0]),
        pltpu.make_async_copy(tokens, buf.at[y, z, c, :, pl.ds(x0, width)], local.at[1]),
        pltpu.make_async_copy(cotangent, buf.at[y, z, c, :, pl.ds(dy0, width)], local.at[2]),
    ]
    weights = [
        pltpu.make_async_copy(w_gate, wg, local.at[3]),
        pltpu.make_async_copy(w_up, wu, local.at[4]),
        pltpu.make_async_copy(w_down, wd, local.at[5]),
    ]
    for copy in loads + weights:
        copy.start()
    for copy in loads:
        copy.wait()
    links.greet(links.plane())

    def piece(start, stop, y_first):
        middle = start + (stop - start) // (2 * LANE) * LANE
        spans = {None: (start, stop), 0: (start, middle), 1: (middle, stop)}

        def at(yy, zz, part):
            low, high = spans[part]
            return buf.at[yy, zz, c, :, pl.ds(low, high - low)]

        return Gather(links, at, y_first)

    half = width // 2
    p0 = piece(0, x0 + half, True)
    p1 = piece(x0 + half, dy0, False)
    p2 = piece(dy0, dy0 + half, True)
    p3 = piece(dy0 + half, end, False)
    p0.one()
    p1.one()
    p0.two()
    p1.two()
    p2.one()
    p3.one()
    p0.three()
    p1.three()
    p2.two()
    p3.two()
    p0.four()
    p1.four()
    p2.three()
    p3.three()
    p0.five()
    p1.five()
    p0.six()
    p1.six()

    for copy in weights:
        copy.wait()
    my_slot = jnp.full((8, 1), me, jnp.int32)
    for g in range(RING):
        part = buf[g, :, :, :, pl.ds(0, LANE)].reshape(line, LANE)
        meta_all[pl.ds(g * line, line), :] = part
        row, gate, _ = entries(part, my_slot, per, cap, top)
        chosen = picks(row[0:1], group_rows)
        select[g] = chosen.astype(BF)
        gate_rows[pl.ds(g * group_rows, group_rows), :] = jnp.broadcast_to(
            jnp.sum(chosen * gate[0:1], axis=1, keepdims=True), (group_rows, LANE)
        )

    chunk = 512

    def fill_rows(start):
        for g in range(RING):
            part = buf[g, :, :, :, pl.ds(start, chunk)].reshape(line, chunk)
            rows_buf[pl.ds(g * group_rows, group_rows), :] = dot(select[g], part).astype(BF)

    gate_acc[...] = jnp.zeros_like(gate_acc)
    up_acc[...] = jnp.zeros_like(up_acc)
    down_acc[...] = jnp.zeros_like(down_acc)

    def x_step(i, carry):
        off = pl.multiple_of(i * chunk, chunk)
        fill_rows(pl.multiple_of(x0 + i * chunk, LANE))
        gate_acc[...] += dot(rows_buf[...], wg[pl.ds(off, chunk), :])
        up_acc[...] += dot(rows_buf[...], wu[pl.ds(off, chunk), :])
        return carry

    def dy_step(i, carry):
        off = pl.multiple_of(i * chunk, chunk)
        fill_rows(pl.multiple_of(dy0 + i * chunk, LANE))
        down_acc[...] += dot(rows_buf[...], wd[pl.ds(off, chunk), :])
        return carry

    steps = width // chunk
    lax.fori_loop(0, steps // 2, x_step, 0)
    p2.four()
    p3.four()
    lax.fori_loop(steps // 2, steps, x_step, 0)
    p2.five()
    p3.five()
    p2.six()
    p3.six()
    lax.fori_loop(0, steps, dy_step, 0)

    own = width // slots
    window = 3 * LANE
    low = jnp.minimum(lax.div(me * own, LANE) * LANE, width - window)
    shift = me * own - low
    move = jnp.where(
        lax.broadcasted_iota(jnp.int32, (window, 2 * LANE), 0)
        == lax.broadcasted_iota(jnp.int32, (window, 2 * LANE), 1) + shift,
        1.0,
        0.0,
    ).astype(BF)
    for k, start in enumerate((x0, dy0)):
        for g in range(RING):
            part = buf[g, :, :, :, pl.ds(pl.multiple_of(start + low, LANE), window)]
            cuts[k, pl.ds(g * line, line), :] = dot(part.reshape(line, window), move).astype(BF)

    def finish(i, carry):
        r = pl.ds(pl.multiple_of(i * 32, 32), 32)
        gate_proj, up_proj, down_proj = gate_acc[r, :], up_acc[r, :], down_acc[r, :]
        sig = jax.nn.sigmoid(gate_proj)
        activated = gate_proj * sig
        hidden = (activated * up_proj).astype(BF)
        hidden_grad = gate_rows[r, 0:1] * down_proj
        acts[r, pl.ds(0, ff)] = (
            hidden_grad * up_proj * sig * (1.0 + gate_proj * (1.0 - sig))
        ).astype(BF)
        acts[r, pl.ds(ff, ff)] = (hidden_grad * activated).astype(BF)
        acts[r, pl.ds(2 * ff, ff)] = hidden
        total = jnp.sum(hidden.astype(F32) * down_proj, axis=1, keepdims=True)
        high = total.astype(BF)
        low_part = (total - high.astype(F32)).astype(BF)
        lanes = lax.broadcasted_iota(jnp.int32, (32, LANE), 1)
        score[r, :] = jnp.where(
            lanes < LANE // 2, high.astype(F32), low_part.astype(F32)
        ).astype(BF)
        return carry

    lax.fori_loop(0, cap * slots // 32, finish, 0)
    links.drain()


def return_kernel(
    dims,
    acts, score, w_gate, w_up,
    acts_all, back,
    wg, wu, a, far, up_buf, down_buf, far_in, sum_in, own_buf, score_in,
    send, recv, local,
):
    per, width, cap, top, ff = dims
    slots = RING * RING * CORES
    rows = cap * slots
    part = width // RING
    half = part // 2
    links = Links(send, recv)
    y, z, c, t = links.y, links.z, links.c, links.t
    own = pltpu.make_async_copy(acts, acts_all.at[y, z, c], local.at[0])
    held = pltpu.make_async_copy(acts, a, local.at[1])
    weights = [
        pltpu.make_async_copy(w_gate, wg, local.at[2]),
        pltpu.make_async_copy(w_up, wu, local.at[3]),
    ]
    for copy in [own, held] + weights:
        copy.start()
    own.wait()
    right, left, across = links.to(t=up1(t)), links.to(t=down1(t)), links.to(t=up1(up1(t)))
    links.greet(links.plane() + [right, left, across])

    def piece(start, stop, y_first):
        middle = (start + stop) // 2
        spans = {None: (start, stop), 0: (start, middle), 1: (middle, stop)}

        def at(yy, zz, which):
            low, high = spans[which]
            return acts_all.at[yy, zz, c, pl.ds(low, high - low), :]

        return Gather(links, at, y_first)

    g0 = piece(0, rows // 2, True)
    g1 = piece(rows // 2, rows, False)
    g0.one()
    g1.one()
    held.wait()
    for copy in weights:
        copy.wait()

    def term(quarter, column):
        r = pl.ds(pl.multiple_of(quarter * part + column, LANE), LANE)
        return dot(a[:, 0:ff], wg[r, :], NT) + dot(a[:, ff : 2 * ff], wu[r, :], NT)

    def fill(out, quarter, low, high, extra=None):
        def step(i, carry):
            column = pl.multiple_of(low + i * LANE, LANE)
            total = term(quarter, column)
            if extra is not None:
                total = total + extra(column)
            out[:, pl.ds(column, LANE)] = total.astype(BF)
            return carry

        lax.fori_loop(0, (high - low) // LANE, step, 0)

    first, second = pl.ds(0, half), pl.ds(half, half)
    fill(far, up1(up1(t)), 0, part)
    f_right = links.start(far.at[:, first], far_in.at[:, first], right)
    f_left = links.start(far.at[:, second], far_in.at[:, second], left)
    g0.two()
    g1.two()
    fill(up_buf, up1(t), half, part)
    d_right = links.start(up_buf.at[:, second], sum_in.at[0, :, second], right)
    fill(down_buf, down1(t), 0, half)
    d_left = links.start(down_buf.at[:, first], sum_in.at[1, :, first], left)
    scores = [
        links.start(score, score_in.at[0], right),
        links.start(score, score_in.at[1], left),
        links.start(score, score_in.at[2], across),
    ]
    g0.three()
    g1.three()
    f_right.wait_recv()
    fill(up_buf, up1(t), 0, half, lambda k: far_in[:, pl.ds(k, LANE)].astype(F32))
    s_right = links.start(up_buf.at[:, first], sum_in.at[0, :, first], right)
    f_left.wait_recv()
    fill(down_buf, down1(t), half, part, lambda k: far_in[:, pl.ds(k, LANE)].astype(F32))
    s_left = links.start(down_buf.at[:, second], sum_in.at[1, :, second], left)
    g0.four()
    g1.four()
    for copy in scores:
        copy.wait_recv()
    total = jnp.zeros((rows, 1), F32)
    for ref in (score, score_in.at[0], score_in.at[1], score_in.at[2]):
        both = ref[...].astype(F32)
        total = total + (both[:, 0:1] + both[:, LANE // 2 : LANE // 2 + 1])
    padded = 16
    spread = jnp.where(
        (
            lax.div(lax.broadcasted_iota(jnp.int32, (slots * padded, rows), 0), padded) * cap
            + lax.rem(lax.broadcasted_iota(jnp.int32, (slots * padded, rows), 0), padded)
            == lax.broadcasted_iota(jnp.int32, (slots * padded, rows), 1)
        )
        & (
            lax.rem(lax.broadcasted_iota(jnp.int32, (slots * padded, rows), 0), padded) < cap
        ),
        1.0,
        0.0,
    ).astype(BF)
    back[:, :, pl.ds(part, LANE)] = (
        dot(spread, jnp.broadcast_to(total, (rows, LANE)).astype(BF))
        .astype(BF)
        .reshape(slots, padded, LANE)
    )
    for copy in (d_right, d_left, s_right, s_left):
        copy.wait_recv()

    def last(i, carry):
        column = pl.multiple_of(i * LANE, LANE)
        cols = pl.ds(column, LANE)
        total = term(t, column) + sum_in[0, :, cols].astype(F32) + sum_in[1, :, cols].astype(F32)
        own_buf[...] = total.astype(BF)
        back[:, :, cols] = dot(spread, own_buf[...]).astype(BF).reshape(slots, padded, LANE)
        return carry

    lax.fori_loop(0, part // LANE, last, 0)
    g0.five()
    g1.five()
    g0.six()
    g1.six()
    links.drain()


def weights_kernel(
    dims, owners, replicas, meta_all, cuts, acts, out, row_at, gate_at, xs, ds_, kept
):
    per, width, cap, top, ff = dims
    slots = RING * RING * CORES
    group_rows = cap * slots // RING
    line = per * slots // RING
    own = width // slots
    i = pl.program_id(0)
    slot = jnp.where(i < replicas, slots - replicas + i, i - replicas)

    @pl.when(i == 0)
    def _():
        ids = lax.broadcasted_iota(jnp.int32, (slots, 1), 0)
        for g in range(RING):
            row, gate, _ = entries(
                meta_all[pl.ds(g * line, line), :], ids, per, cap, top
            )
            row_at[g] = row
            gate_at[g] = gate

    for g in range(RING):
        chosen = picks(row_at[g, pl.ds(slot, 1), :], group_rows)
        weighed = chosen * gate_at[g, pl.ds(slot, 1), :]
        toks = pl.ds(g * line, line)
        rows = pl.ds(g * group_rows, group_rows)
        xs[rows, :] = dot(chosen.astype(BF), cuts[0, toks, :]).astype(BF)
        ds_[rows, :] = dot(weighed.astype(BF), cuts[1, toks, :]).astype(BF)
    in_grads = dot(xs[...], acts[0, :, 0 : 2 * ff], TN)
    down = dot(ds_[...], acts[0, :, 2 * ff :], TN)
    parts = (in_grads[:own, :ff], in_grads[:own, ff:], down[:own])

    @pl.when(i < replicas)
    def _():
        for k in range(3):
            kept[i, k] = parts[k]

    @pl.when(i >= replicas)
    def _():
        expert = i - replicas
        owned = owners[0] == expert
        for r in range(1, replicas):
            owned = owned | (owners[r] == expert)

        @pl.when(jnp.logical_not(owned))
        def _():
            for k in range(3):
                out[0, k] = parts[k].astype(BF)

        @pl.when(owned)
        def _():
            for k in range(3):
                total = parts[k]
                for r in range(replicas):
                    total = total + jnp.where(owners[r] == expert, kept[r, k], 0.0)
                out[0, k] = total.astype(BF)


def tokens_kernel(dims, meta, back, input_grads, gate_grads):
    per, width, cap, top, ff = dims
    slots = RING * RING * CORES
    part = width // RING
    padded = back.shape[1]
    ids = lax.broadcasted_iota(jnp.int32, (slots, 1), 0)
    row, _, turned = entries(meta[...], ids, per, cap, top)
    place = lax.broadcasted_iota(jnp.int32, (slots, padded, LANE), 1).astype(F32)
    chosen = jnp.where(row[:, None, :] == place, 1.0, 0.0)
    flat = chosen.reshape(slots * padded, LANE).astype(BF)
    for k in range(part // (2 * LANE)):
        cols = pl.ds(k * 2 * LANE, 2 * LANE)
        rows = back[:, :, cols].reshape(slots * padded, 2 * LANE)
        input_grads[:, cols] = dot(flat, rows, TN)[:per].astype(BF)
    score = back[:, :, pl.ds(part, LANE)].astype(F32)
    by_slot = jnp.sum(chosen * score, axis=1)
    for k in range(top):
        same = turned[k : k + 1] == ids.astype(F32)
        line = jnp.sum(jnp.where(same, by_slot, 0.0), axis=0, keepdims=True)
        gate_grads[pl.ds(k, 1), :] = line[:, :per]


def per_device(tokens, cotangent, gate_weights, route_slots, replica_owner, w_gate, w_up, w_down):
    slots = lax.axis_size("expert")
    per, width = tokens.shape
    top = route_slots.shape[1]
    cap = per * top * 3 // 2 // slots
    ff = w_gate.shape[2]
    rows = cap * slots
    part = width // RING
    padded = 16
    replicas = replica_owner.shape[0]
    experts = slots - replicas
    dims = (per, width, cap, top, ff)
    meta = jnp.concatenate(
        [
            route_slots.astype(BF),
            gate_weights,
            jnp.full((per, LANE - 2 * top), -1, BF),
        ],
        axis=1,
    )
    w_gate, w_up, w_down = w_gate[0], w_up[0], w_down[0]
    any_ = pl.BlockSpec(memory_space=pl.ANY)
    vmem = pl.BlockSpec(memory_space=pltpu.VMEM)
    line = per * slots // RING
    copies = 4 * GATHER_COPIES
    acts, score, cuts, meta_all = pl.pallas_call(
        functools.partial(dispatch_kernel, dims),
        name="dispatch",
        out_shape=(
            jax.ShapeDtypeStruct((rows, 3 * ff), BF),
            jax.ShapeDtypeStruct((rows, LANE), BF),
            jax.ShapeDtypeStruct((2, per * slots, 2 * LANE), BF),
            jax.ShapeDtypeStruct((per * slots, LANE), BF),
        ),
        in_specs=[any_] * 6,
        out_specs=(vmem,) * 4,
        scratch_shapes=[
            pltpu.VMEM((RING, RING, CORES, per, LANE + 2 * width), BF),
            pltpu.VMEM((width, ff), BF),
            pltpu.VMEM((width, ff), BF),
            pltpu.VMEM((width, ff), BF),
            pltpu.VMEM((rows, 512), BF),
            pltpu.VMEM((rows, ff), F32),
            pltpu.VMEM((rows, ff), F32),
            pltpu.VMEM((rows, ff), F32),
            pltpu.VMEM((RING, rows // RING, line), BF),
            pltpu.VMEM((rows, LANE), F32),
            pltpu.SemaphoreType.DMA((copies,)),
            pltpu.SemaphoreType.DMA((copies,)),
            pltpu.SemaphoreType.DMA((6,)),
        ],
        compiler_params=pltpu.CompilerParams(
            collective_id=0, has_side_effects=True, vmem_limit_bytes=56 * MIB
        ),
    )(tokens, cotangent, meta, w_gate, w_up, w_down)
    copies = 2 * GATHER_COPIES + 9
    acts_all, back = pl.pallas_call(
        functools.partial(return_kernel, dims),
        name="activations_out",
        out_shape=(
            jax.ShapeDtypeStruct((RING, RING, CORES, rows, 3 * ff), BF),
            jax.ShapeDtypeStruct((slots, padded, part + LANE), BF),
        ),
        in_specs=[any_, vmem, any_, any_],
        out_specs=(any_, vmem),
        scratch_shapes=[
            pltpu.VMEM((width, ff), BF),
            pltpu.VMEM((width, ff), BF),
            pltpu.VMEM((rows, 3 * ff), BF),
            pltpu.VMEM((rows, part), BF),
            pltpu.VMEM((rows, part), BF),
            pltpu.VMEM((rows, part), BF),
            pltpu.VMEM((rows, part), BF),
            pltpu.VMEM((2, rows, part), BF),
            pltpu.VMEM((rows, LANE), BF),
            pltpu.VMEM((3, rows, LANE), BF),
            pltpu.SemaphoreType.DMA((copies,)),
            pltpu.SemaphoreType.DMA((copies,)),
            pltpu.SemaphoreType.DMA((4,)),
        ],
        compiler_params=pltpu.CompilerParams(
            collective_id=1, has_side_effects=True, vmem_limit_bytes=56 * MIB
        ),
    )(acts, score, w_gate, w_up)
    returned = lax.all_to_all(back, "expert", 0, 0, tiled=True)
    own = width // slots
    expert_grads = pl.pallas_call(
        lambda owners, *refs: weights_kernel(dims, owners, replicas, *refs),
        name="weight_grads",
        out_shape=jax.ShapeDtypeStruct((experts, 3, own, ff), BF),
        grid_spec=pltpu.PrefetchScalarGridSpec(
            num_scalar_prefetch=1,
            grid=(slots,),
            in_specs=[
                pl.BlockSpec((per * slots, LANE), lambda i, o: (0, 0)),
                pl.BlockSpec((2, per * slots, 2 * LANE), lambda i, o: (0, 0, 0)),
                pl.BlockSpec(
                    (1, rows, 3 * ff),
                    lambda i, o: (jnp.where(i < replicas, experts + i, i - replicas), 0, 0),
                ),
            ],
            out_specs=pl.BlockSpec(
                (1, 3, own, ff), lambda i, o: (jnp.maximum(i - replicas, 0), 0, 0, 0)
            ),
            scratch_shapes=[
                pltpu.VMEM((RING, slots, line), F32),
                pltpu.VMEM((RING, slots, line), F32),
                pltpu.VMEM((rows, 2 * LANE), BF),
                pltpu.VMEM((rows, 2 * LANE), BF),
                pltpu.VMEM((replicas, 3, own, ff), F32),
            ],
        ),
        compiler_params=pltpu.CompilerParams(vmem_limit_bytes=40 * MIB),
        cost_estimate=pl.CostEstimate(
            flops=8_000_000_000, bytes_accessed=32_000_000, transcendentals=0
        ),
    )(replica_owner, meta_all, cuts, acts_all.reshape(slots, rows, 3 * ff))
    own_meta = jnp.concatenate([meta, jnp.full((LANE - per, LANE), -1, BF)], axis=0)
    input_grads, gate_grads = pl.pallas_call(
        functools.partial(tokens_kernel, dims),
        name="token_grads",
        out_shape=(
            jax.ShapeDtypeStruct((per, part), BF),
            jax.ShapeDtypeStruct((top, per), F32),
        ),
        in_specs=[vmem, vmem],
        out_specs=(vmem, vmem),
        compiler_params=pltpu.CompilerParams(vmem_limit_bytes=32 * MIB),
    )(own_meta, returned)
    return (
        input_grads,
        jnp.transpose(gate_grads.astype(BF)),
        jnp.transpose(expert_grads, (0, 2, 1, 3)),
    )


def solution(mesh):
    in_specs = (
        P("expert", None),
        P("expert", None),
        P("expert", None),
        P("expert", None),
        P(),
        P("expert", None, "tensor"),
        P("expert", None, "tensor"),
        P("expert", None, "tensor"),
    )
    out_specs = (P("expert", "tensor"), P("expert", None), P(None, "expert", None, "tensor"))
    return jax.shard_map(
        per_device, mesh=mesh, in_specs=in_specs, out_specs=out_specs, check_vma=False
    )
```

profile of v0, /device:TPU:1, one launch (start us, length us, event | category | flops | bytes accessed | tf_op | source)
XLA Modules:
  0.0 235.0 jit_solution(15820476014575138472)
XLA Ops:
  0.6 0.8 copy.14
  1.4 0.7 convert_element_type.6
  2.1 0.1 copy.13
  2.2 0.1 pad.3.clone
  2.3 0.7 maximum_maximum_fusion.meta
  2.9 99.6 %dispatch.1 = (bf16[384,768]{1,0:T(8,128)(2,1)}, bf16[384,128]{1,0:T(8,128)(2,1)}, bf16[2,1024,256]{2,1,0:T(8,128)(2,1)}, bf16[1024,128]{1,0:T(8,128)(2,1)}) custom-call(bf16[32,7168]{1,0:T(8,128)(2,1)} %tokens.1, bf16[32,7168]{1,0:T(8,128)(2,1)} %cotangent.1, bf16[32,128]{1,0:T(8,128)(2,1)} %maximum_maximum_fusion.meta, bf16[7168,256]{1,0:T(8,128)(2,1)} %bitcast.8, ...), custom_call_target="tpu_custom_call" | custom-call | tf_op jit(solution)/shard_map/dispatch/pallas_call | solution.py:570
  102.5 91.2 %activations_out.1 = (bf16[4,4,2,384,768]{4,3,2,1,0:T(8,128)(2,1)}, bf16[32,16,1920]{2,1,0:T(8,128)(2,1)}) custom-call(bf16[384,768]{1,0:T(8,128)(2,1)} %get-tuple-element.11.acts, bf16[384,128]{1,0:T(8,128)(2,1)} %get-tuple-element.12.score, bf16[7168,256]{1,0:T(8,128)(2,1)} %bitcast.9, bf16[7168,256]{1,0:T(8,128)(2,1)} %bitcast.11), custom_call_target="tpu_custom_call" | custom-call | tf_op jit(solution)/shard_map/activations_out/pallas_call | solution.py:601
  193.7 0.0 copy-start.3
  193.7 0.0 copy-start
  193.8 0.0 copy-start.1
  193.8 0.0 copy-start.2
  193.8 5.7 %all-to-all-start = ((bf16[32,16,1920]{2,1,0:T(8,128)(2,1)}), bf16[32,16,1920]{2,1,0:T(8,128)(2,1)S(1)}, u32[]{:S(2)}, u32[]{:S(2)}) async-start(bf16[32,16,1920]{2,1,0:T(8,128)(2,1)} %get-tuple-element.13), calls=%async_computation | async-start | bytes 3932160 | tf_op jit(solution)/shard_map/all_to_all | solution.py:629
  199.4 0.0 copy-done.3
  199.5 0.0 copy-done
  199.5 0.0 copy-done.1
  199.5 0.0 copy-done.2
  199.5 33.5 %weight_grads.1 = bf16[28,3,224,256]{3,2,1,0:T(8,128)(2,1)} custom-call(s32[4]{0:T(128)S(1)} %copy-done.2, bf16[1024,128]{1,0:T(8,128)(2,1)S(1)} %copy-done.1, bf16[2,1024,256]{2,1,0:T(8,128)(2,1)S(1)} %copy-done, bf16[32,384,768]{2,1,0:T(8,128)(2,1)} %bitcast.7), custom_call_target="tpu_custom_call" | custom-call | flops 8000000000 | bytes 32000000 | tf_op jit(solution)/shard_map/weight_grads/pallas_call | solution.py:631
  233.0 0.0 all-to-all-done.back
  233.0 1.4 token_grads.1
  234.4 0.6 convert_bitcast_fusion
  (2 shorter events, 0.0 us)
Async XLA Ops:
  193.7 5.7 %copy-start.3 = (bf16[32,128]{1,0:T(8,128)(2,1)S(1)}, bf16[32,128]{1,0:T(8,128)(2,1)}, u32[]{:S(2)}) copy-start(bf16[32,128]{1,0:T(8,128)(2,1)} %maximum_maximum_fusion.meta) | copy-start | bytes 24580
  193.7 5.7 %copy-start = (bf16[2,1024,256]{2,1,0:T(8,128)(2,1)S(1)}, bf16[2,1024,256]{2,1,0:T(8,128)(2,1)}, u32[]{:S(2)}) copy-start(bf16[2,1024,256]{2,1,0:T(8,128)(2,1)} %get-tuple-element.17.refs_1_) | copy-start | bytes 3145732
  193.8 5.7 %copy-start.1 = (bf16[1024,128]{1,0:T(8,128)(2,1)S(1)}, bf16[1024,128]{1,0:T(8,128)(2,1)}, u32[]{:S(2)}) copy-start(bf16[1024,128]{1,0:T(8,128)(2,1)} %get-tuple-element.16.refs_0_) | copy-start | bytes 786436
  193.8 5.7 %copy-start.2 = (s32[4]{0:T(128)S(1)}, s32[4]{0:T(128)}, u32[]{:S(2)}) copy-start(s32[4]{0:T(128)} %owners.1) | copy-start | bytes 52
  193.8 39.2 %all-to-all-start = ((bf16[32,16,1920]{2,1,0:T(8,128)(2,1)}), bf16[32,16,1920]{2,1,0:T(8,128)(2,1)S(1)}, u32[]{:S(2)}, u32[]{:S(2)}) async-start(bf16[32,16,1920]{2,1,0:T(8,128)(2,1)} %get-tuple-element.13), calls=%async_computation | async-start | bytes 3932160 | tf_op jit(solution)/shard_map/all_to_all | solution.py:629
where the time goes:
time: 236 us; the launch traced here: 235 us
  Pallas kernels  226 us (96%)
  starting transfers between devices  5.67 us (2%)
    pallas_call x1, Pallas kernels, per_device(): pl.pallas_call(functools.partial(dispatch_kernel, dims), name='dispatch',...  99.6 us
    pallas_call x1, Pallas kernels, per_device(): pl.pallas_call(functools.partial(return_kernel, dims), name='activations_...  91.2 us
    pallas_call x1, Pallas kernels, per_device(): pl.pallas_call(lambda owners, *refs: weights_kernel(dims, owners, replica...  33.5 us
    all_to_all x1, starting transfers between devices, per_device(): returned = lax.all_to_all(back, 'expert', 0, 0, tiled=True)  5.67 us
  transfers between devices with their start and end apart: 1, of which 0 were waited for; matrix products, arithmetic and copies ran while one was open for 0% of the time, Pallas kernels for 14%

commit v1 on v0

--- a/solution.py
+++ b/solution.py
@@ -11,6 +11,7 @@
 BF = jnp.bfloat16
 F32 = jnp.float32
 LANE = 128
+SHARED = 6
 RING = 4
 CORES = 2
 MIB = 1 << 20
@@ -85,8 +86,8 @@
 
 
 class Gather:
-    def __init__(self, links, at, y_first):
-        self.l, self.at, self.y_first = links, at, y_first
+    def __init__(self, links, at, y_first, handed=True):
+        self.l, self.at, self.y_first, self.handed = links, at, y_first, handed
         self.first = links.y if y_first else links.z
         self.second = links.z if y_first else links.y
 
@@ -103,8 +104,13 @@
         return self.l.start(ref, ref, device)
 
     def hand_over(self, second):
-        ref = self.place(slice(None), second)
-        return self.copy(ref, self.l.to(c=1 - self.l.c))
+        if self.handed:
+            ref = self.place(slice(None), second)
+            self.s.append(self.copy(ref, self.l.to(c=1 - self.l.c)))
+
+    def lines(self):
+        low, high = down1(self.second), up1(self.second)
+        return [self.second, low, high, up1(high)]
 
     def one(self):
         own = self.place(self.first, self.second)
@@ -127,21 +133,22 @@
         line = self.place(slice(None), self.second)
         self.m5 = self.copy(line, self.along_second(up1(self.second)))
         self.m6 = self.copy(line, self.along_second(down1(self.second)))
-        self.s = [self.hand_over(self.second)]
+        self.s = []
+        self.hand_over(self.second)
 
     def four(self):
         low, high = down1(self.second), up1(self.second)
         self.m5.wait_recv()
         self.m7 = self.copy(self.place(slice(None), low, 0), self.along_second(high))
-        self.s.append(self.hand_over(low))
+        self.hand_over(low)
         self.m6.wait_recv()
         self.m8 = self.copy(self.place(slice(None), high, 1), self.along_second(low))
-        self.s.append(self.hand_over(high))
+        self.hand_over(high)
 
     def five(self):
         self.m7.wait_recv()
         self.m8.wait_recv()
-        self.s.append(self.hand_over(up1(up1(self.second))))
+        self.hand_over(up1(up1(self.second)))
 
     def six(self):
         for copy in self.s:
@@ -149,6 +156,37 @@
 
 
 GATHER_COPIES = 12
+
+
+class Across:
+    def __init__(self, links, at, whole):
+        self.l, self.at, self.whole = links, at, whole
+
+    def copy(self, ref, device):
+        return self.l.start(ref, ref, device)
+
+    def one(self):
+        t = self.l.t
+        self.m1 = self.copy(self.at(t), self.l.to(t=up1(t)))
+        self.m2 = self.copy(self.at(t), self.l.to(t=down1(t)))
+
+    def two(self):
+        t = self.l.t
+        self.m1.wait_recv()
+        self.m3 = self.copy(self.at(down1(t), 0), self.l.to(t=up1(t)))
+        self.m2.wait_recv()
+        self.m4 = self.copy(self.at(up1(t), 1), self.l.to(t=down1(t)))
+
+    def three(self):
+        self.m3.wait_recv()
+        self.m4.wait_recv()
+        self.s = self.copy(self.whole, self.l.to(c=1 - self.l.c))
+
+    def four(self):
+        self.s.wait_recv()
+
+
+ACROSS_COPIES = 5
 
 
 def entries(meta, slot, per, cap, top):
@@ -211,39 +249,97 @@
         copy.start()
     for copy in loads:
         copy.wait()
-    links.greet(links.plane())
-
-    def piece(start, stop, y_first):
-        middle = start + (stop - start) // (2 * LANE) * LANE
-        spans = {None: (start, stop), 0: (start, middle), 1: (middle, stop)}
+    t = links.t
+    links.greet(links.plane() + [links.to(t=up1(t)), links.to(t=down1(t))])
+
+    def piece(start, size, y_first, handed=True):
+        middle = size // (2 * LANE) * LANE
+        spans = {None: (0, size), 0: (0, middle), 1: (middle, size - middle)}
 
         def at(yy, zz, part):
-            low, high = spans[part]
-            return buf.at[yy, zz, c, :, pl.ds(low, high - low)]
-
-        return Gather(links, at, y_first)
-
-    half = width // 2
+            low, count = spans[part]
+            return buf.at[yy, zz, c, :, pl.ds(pl.multiple_of(start + low, LANE), count)]
+
+        return Gather(links, at, y_first, handed)
+
+    quarter = SHARED * LANE
+    straight = width - RING * quarter
+    half = straight // 2
+
+    def across(first, gather):
+        def ring(line):
+            def at(owner, part=None):
+                low, count = {
+                    None: (0, quarter),
+                    0: (0, quarter // 2),
+                    1: (quarter // 2, quarter // 2),
+                }[part]
+                cols = pl.ds(pl.multiple_of(first + owner * quarter + low, LANE), count)
+                if gather.y_first:
+                    return buf.at[:, line, c, :, cols]
+                return buf.at[line, :, c, :, cols]
+
+            cols = pl.ds(first, RING * quarter)
+            if gather.y_first:
+                whole = buf.at[:, line, c, :, cols]
+            else:
+                whole = buf.at[line, :, c, :, cols]
+            return Across(links, at, whole)
+
+        return [ring(line) for line in gather.lines()]
+
+    qx0, qdy0 = x0 + straight, dy0 + straight
+    qa = piece(qx0 + t * quarter, quarter, True, False)
+    qb = piece(qdy0 + t * quarter, quarter, False, False)
+    xa, xb = across(qx0, qa), across(qdy0, qb)
     p0 = piece(0, x0 + half, True)
-    p1 = piece(x0 + half, dy0, False)
-    p2 = piece(dy0, dy0 + half, True)
-    p3 = piece(dy0 + half, end, False)
+    p1 = piece(x0 + half, half, False)
+    p2 = piece(dy0, half, True)
+    p3 = piece(dy0 + half, half, False)
+    qa.one()
+    qb.one()
+    qa.two()
+    qb.two()
     p0.one()
     p1.one()
+    qa.three()
+    xa[0].one()
+    qb.three()
+    xb[0].one()
     p0.two()
     p1.two()
+    qa.four()
+    xa[1].one()
+    xa[2].one()
+    qb.four()
+    p0.three()
+    p1.three()
+    qa.five()
+    xa[3].one()
+    qb.five()
     p2.one()
     p3.one()
-    p0.three()
-    p1.three()
+    xa[0].two()
+    xb[1].one()
+    xb[2].one()
     p2.two()
     p3.two()
+    xa[1].two()
+    xa[2].two()
+    xb[3].one()
     p0.four()
     p1.four()
     p2.three()
     p3.three()
+    xa[3].two()
+    xa[0].three()
+    xb[0].two()
     p0.five()
     p1.five()
+    xa[1].three()
+    xa[2].three()
+    xb[1].two()
+    xb[2].two()
     p0.six()
     p1.six()
 
@@ -284,17 +380,6 @@
         down_acc[...] += dot(rows_buf[...], wd[pl.ds(off, chunk), :])
         return carry
 
-    steps = width // chunk
-    lax.fori_loop(0, steps // 2, x_step, 0)
-    p2.four()
-    p3.four()
-    lax.fori_loop(steps // 2, steps, x_step, 0)
-    p2.five()
-    p3.five()
-    p2.six()
-    p3.six()
-    lax.fori_loop(0, steps, dy_step, 0)
-
     own = width // slots
     window = 3 * LANE
     low = jnp.minimum(lax.div(me * own, LANE) * LANE, width - window)
@@ -305,42 +390,76 @@
         1.0,
         0.0,
     ).astype(BF)
-    for k, start in enumerate((x0, dy0)):
+
+    def cut(k, start):
         for g in range(RING):
             part = buf[g, :, :, :, pl.ds(pl.multiple_of(start + low, LANE), window)]
             cuts[k, pl.ds(g * line, line), :] = dot(part.reshape(line, window), move).astype(BF)
 
-    def finish(i, carry):
-        r = pl.ds(pl.multiple_of(i * 32, 32), 32)
-        gate_proj, up_proj, down_proj = gate_acc[r, :], up_acc[r, :], down_acc[r, :]
+    strip = 32
+
+    def silu_step(i, carry):
+        r = pl.ds(pl.multiple_of(i * strip, strip), strip)
+        gate_proj, up_proj = gate_acc[r, :], up_acc[r, :]
         sig = jax.nn.sigmoid(gate_proj)
         activated = gate_proj * sig
-        hidden = (activated * up_proj).astype(BF)
+        acts[r, pl.ds(2 * ff, ff)] = (activated * up_proj).astype(BF)
+        gate_acc[r, :] = up_proj * sig * (1.0 + gate_proj * (1.0 - sig))
+        up_acc[r, :] = activated
+        return carry
+
+    def finish(i, carry):
+        r = pl.ds(pl.multiple_of(i * strip, strip), strip)
+        down_proj = down_acc[r, :]
         hidden_grad = gate_rows[r, 0:1] * down_proj
-        acts[r, pl.ds(0, ff)] = (
-            hidden_grad * up_proj * sig * (1.0 + gate_proj * (1.0 - sig))
-        ).astype(BF)
-        acts[r, pl.ds(ff, ff)] = (hidden_grad * activated).astype(BF)
-        acts[r, pl.ds(2 * ff, ff)] = hidden
-        total = jnp.sum(hidden.astype(F32) * down_proj, axis=1, keepdims=True)
+        acts[r, pl.ds(0, ff)] = (hidden_grad * gate_acc[r, :]).astype(BF)
+        acts[r, pl.ds(ff, ff)] = (hidden_grad * up_acc[r, :]).astype(BF)
+        hidden = acts[r, pl.ds(2 * ff, ff)].astype(F32)
+        total = jnp.sum(hidden * down_proj, axis=1, keepdims=True)
         high = total.astype(BF)
         low_part = (total - high.astype(F32)).astype(BF)
-        lanes = lax.broadcasted_iota(jnp.int32, (32, LANE), 1)
+        lanes = lax.broadcasted_iota(jnp.int32, (strip, LANE), 1)
         score[r, :] = jnp.where(
             lanes < LANE // 2, high.astype(F32), low_part.astype(F32)
         ).astype(BF)
         return carry
 
-    lax.fori_loop(0, cap * slots // 32, finish, 0)
+    steps, plain = width // chunk, straight // chunk
+    strips = cap * slots // strip
+    lax.fori_loop(0, plain, x_step, 0)
+    p2.four()
+    p3.four()
+    xa[3].three()
+    xb[0].three()
+    xb[3].two()
+    for ring in xa:
+        ring.four()
+    lax.fori_loop(plain, steps, x_step, 0)
+    xb[1].three()
+    xb[2].three()
+    cut(0, x0)
+    lax.fori_loop(0, strips, silu_step, 0)
+    p2.five()
+    p3.five()
+    xb[3].three()
+    p2.six()
+    p3.six()
+    lax.fori_loop(0, plain, dy_step, 0)
+    for ring in xb:
+        ring.four()
+    lax.fori_loop(plain, steps, dy_step, 0)
+    cut(1, dy0)
+    lax.fori_loop(0, strips, finish, 0)
     links.drain()
 
 
 def return_kernel(
     dims,
-    acts, score, w_gate, w_up,
-    acts_all, back,
-    wg, wu, a, far, up_buf, down_buf, far_in, sum_in, own_buf, score_in,
-    send, recv, local,
+    acts, score, meta_all, cuts, w_gate, w_up,
+    acts_all, turned_all, back,
+    held_all, wg, wu, a, far, up_buf, down_buf, far_in, sum_in, own_buf, score_in,
+    row_at, gate_at, rows_buf, turned,
+    send, recv, local, out_sem,
 ):
     per, width, cap, top, ff = dims
     slots = RING * RING * CORES
@@ -349,7 +468,7 @@
     half = part // 2
     links = Links(send, recv)
     y, z, c, t = links.y, links.z, links.c, links.t
-    own = pltpu.make_async_copy(acts, acts_all.at[y, z, c], local.at[0])
+    own = pltpu.make_async_copy(acts, held_all.at[y, z, c], local.at[0])
     held = pltpu.make_async_copy(acts, a, local.at[1])
     weights = [
         pltpu.make_async_copy(w_gate, wg, local.at[2]),
@@ -367,9 +486,56 @@
 
         def at(yy, zz, which):
             low, high = spans[which]
-            return acts_all.at[yy, zz, c, pl.ds(low, high - low), :]
+            return held_all.at[yy, zz, c, pl.ds(low, high - low), :]
 
         return Gather(links, at, y_first)
+
+    outs = []
+
+    def copy_out(gather, index, core):
+        line = gather.lines()[index]
+        r = pl.ds(0, rows // 2) if gather.y_first else pl.ds(rows // 2, rows // 2)
+        if gather.y_first:
+            src, dst = held_all.at[:, line, core, r, :], acts_all.at[:, line, core, r, :]
+        else:
+            src, dst = held_all.at[line, :, core, r, :], acts_all.at[line, :, core, r, :]
+        outs.append(pltpu.make_async_copy(src, dst, out_sem.at[len(outs)]))
+        outs[-1].start()
+
+    group_rows = rows // RING
+    line_tokens = per * slots // RING
+    width_own = width // slots
+
+    def place_rows():
+        ids = lax.broadcasted_iota(jnp.int32, (slots, 1), 0)
+        for g in range(RING):
+            row, gate, _ = entries(
+                meta_all[pl.ds(g * line_tokens, line_tokens), :], ids, per, cap, top
+            )
+            row_at[g] = row
+            gate_at[g] = gate
+
+    several = 4
+
+    def turn_step(i, carry):
+        for g in range(RING):
+            toks = pl.ds(g * line_tokens, line_tokens)
+            chosen, weighed = [], []
+            for j in range(several):
+                slot = i * several + j
+                pick = picks(row_at[g, pl.ds(slot, 1), :], group_rows)
+                chosen.append(pick.astype(BF))
+                weighed.append((pick * gate_at[g, pl.ds(slot, 1), :]).astype(BF))
+            for k, lhs in enumerate((chosen, weighed)):
+                found = dot(jnp.concatenate(lhs, axis=0), cuts[k, toks, :])
+                for j in range(several):
+                    rows_buf[j, k, pl.ds(g * group_rows, group_rows), :] = found[
+                        j * group_rows : (j + 1) * group_rows
+                    ].astype(BF)
+        for j in range(several):
+            for k in range(2):
+                turned[i * several + j, k] = jnp.transpose(rows_buf[j, k])[:width_own]
+        return carry
 
     g0 = piece(0, rows // 2, True)
     g1 = piece(rows // 2, rows, False)
@@ -409,16 +575,25 @@
         links.start(score, score_in.at[1], left),
         links.start(score, score_in.at[2], across),
     ]
+    place_rows()
     g0.three()
     g1.three()
+    copy_out(g0, 0, c)
+    copy_out(g1, 0, c)
     f_right.wait_recv()
     fill(up_buf, up1(t), 0, half, lambda k: far_in[:, pl.ds(k, LANE)].astype(F32))
     s_right = links.start(up_buf.at[:, first], sum_in.at[0, :, first], right)
     f_left.wait_recv()
     fill(down_buf, down1(t), half, part, lambda k: far_in[:, pl.ds(k, LANE)].astype(F32))
     s_left = links.start(down_buf.at[:, second], sum_in.at[1, :, second], left)
+    lax.fori_loop(0, slots // several, turn_step, 0)
+    turned_out = pltpu.make_async_copy(turned, turned_all, local.at[4])
+    turned_out.start()
     g0.four()
     g1.four()
+    for gather in (g0, g1):
+        copy_out(gather, 1, c)
+        copy_out(gather, 2, c)
     for copy in scores:
         copy.wait_recv()
     total = jnp.zeros((rows, 1), F32)
@@ -457,67 +632,50 @@
     lax.fori_loop(0, part // LANE, last, 0)
     g0.five()
     g1.five()
-    g0.six()
-    g1.six()
+    for gather in (g0, g1):
+        copy_out(gather, 3, c)
+    for gather in (g0, g1):
+        gather.six()
+        for index in range(RING):
+            copy_out(gather, index, 1 - c)
     links.drain()
-
-
-def weights_kernel(
-    dims, owners, replicas, meta_all, cuts, acts, out, row_at, gate_at, xs, ds_, kept
-):
-    per, width, cap, top, ff = dims
-    slots = RING * RING * CORES
-    group_rows = cap * slots // RING
-    line = per * slots // RING
-    own = width // slots
+    turned_out.wait()
+    for copy in outs:
+        copy.wait()
+
+
+def weights_kernel(dims, owners, replicas, turned, acts, out, kept):
+    ff = dims[-1]
     i = pl.program_id(0)
-    slot = jnp.where(i < replicas, slots - replicas + i, i - replicas)
+
+    def parts(j):
+        in_grads = dot(turned[j, 0], acts[j, :, 0 : 2 * ff])
+        down = dot(turned[j, 1], acts[j, :, 2 * ff :])
+        return in_grads[:, :ff], in_grads[:, ff:], down
 
     @pl.when(i == 0)
     def _():
-        ids = lax.broadcasted_iota(jnp.int32, (slots, 1), 0)
-        for g in range(RING):
-            row, gate, _ = entries(
-                meta_all[pl.ds(g * line, line), :], ids, per, cap, top
-            )
-            row_at[g] = row
-            gate_at[g] = gate
-
-    for g in range(RING):
-        chosen = picks(row_at[g, pl.ds(slot, 1), :], group_rows)
-        weighed = chosen * gate_at[g, pl.ds(slot, 1), :]
-        toks = pl.ds(g * line, line)
-        rows = pl.ds(g * group_rows, group_rows)
-        xs[rows, :] = dot(chosen.astype(BF), cuts[0, toks, :]).astype(BF)
-        ds_[rows, :] = dot(weighed.astype(BF), cuts[1, toks, :]).astype(BF)
-    in_grads = dot(xs[...], acts[0, :, 0 : 2 * ff], TN)
-    down = dot(ds_[...], acts[0, :, 2 * ff :], TN)
-    parts = (in_grads[:own, :ff], in_grads[:own, ff:], down[:own])
-
-    @pl.when(i < replicas)
+        for j in range(replicas):
+            for k, part in enumerate(parts(j)):
+                kept[j, k] = part
+
+    @pl.when(i > 0)
     def _():
-        for k in range(3):
-            kept[i, k] = parts[k]
-
-    @pl.when(i >= replicas)
-    def _():
-        expert = i - replicas
-        owned = owners[0] == expert
-        for r in range(1, replicas):
-            owned = owned | (owners[r] == expert)
-
-        @pl.when(jnp.logical_not(owned))
-        def _():
-            for k in range(3):
-                out[0, k] = parts[k].astype(BF)
-
-        @pl.when(owned)
-        def _():
-            for k in range(3):
-                total = parts[k]
-                for r in range(replicas):
-                    total = total + jnp.where(owners[r] == expert, kept[r, k], 0.0)
-                out[0, k] = total.astype(BF)
+        for j in range(replicas):
+            for k, part in enumerate(parts(j)):
+                out[j, k] = part.astype(BF)
+            expert = (i - 1) * replicas + j
+            owned = owners[0] == expert
+            for r in range(1, replicas):
+                owned = owned | (owners[r] == expert)
+
+            @pl.when(owned)
+            def _():
+                for k in range(3):
+                    total = out[j, k].astype(F32)
+                    for r in range(replicas):
+                        total = total + jnp.where(owners[r] == expert, kept[r, k], 0.0)
+                    out[j, k] = total.astype(BF)
 
 
 def tokens_kernel(dims, meta, back, input_grads, gate_grads):
@@ -566,7 +724,7 @@
     any_ = pl.BlockSpec(memory_space=pl.ANY)
     vmem = pl.BlockSpec(memory_space=pltpu.VMEM)
     line = per * slots // RING
-    copies = 4 * GATHER_COPIES
+    copies = 4 * GATHER_COPIES + 2 * (GATHER_COPIES - 4) + 8 * ACROSS_COPIES
     acts, score, cuts, meta_all = pl.pallas_call(
         functools.partial(dispatch_kernel, dims),
         name="dispatch",
@@ -598,16 +756,19 @@
         ),
     )(tokens, cotangent, meta, w_gate, w_up, w_down)
     copies = 2 * GATHER_COPIES + 9
-    acts_all, back = pl.pallas_call(
+    own = width // slots
+    acts_all, turned_all, back = pl.pallas_call(
         functools.partial(return_kernel, dims),
         name="activations_out",
         out_shape=(
             jax.ShapeDtypeStruct((RING, RING, CORES, rows, 3 * ff), BF),
+            jax.ShapeDtypeStruct((slots, 2, own, rows), BF),
             jax.ShapeDtypeStruct((slots, padded, part + LANE), BF),
         ),
-        in_specs=[any_, vmem, any_, any_],
-        out_specs=(any_, vmem),
+        in_specs=[any_, vmem, vmem, vmem, any_, any_],
+        out_specs=(any_, any_, vmem),
         scratch_shapes=[
+            pltpu.VMEM((RING, RING, CORES, rows, 3 * ff), BF),
             pltpu.VMEM((width, ff), BF),
             pltpu.VMEM((width, ff), BF),
             pltpu.VMEM((rows, 3 * ff), BF),
@@ -618,47 +779,47 @@
             pltpu.VMEM((2, rows, part), BF),
             pltpu.VMEM((rows, LANE), BF),
             pltpu.VMEM((3, rows, LANE), BF),
+            pltpu.VMEM((RING, slots, line), F32),
+            pltpu.VMEM((RING, slots, line), F32),
+            pltpu.VMEM((4, 2, rows, 2 * LANE), BF),
+            pltpu.VMEM((slots, 2, own, rows), BF),
             pltpu.SemaphoreType.DMA((copies,)),
             pltpu.SemaphoreType.DMA((copies,)),
-            pltpu.SemaphoreType.DMA((4,)),
+            pltpu.SemaphoreType.DMA((5,)),
+            pltpu.SemaphoreType.DMA((4 * RING,)),
         ],
         compiler_params=pltpu.CompilerParams(
-            collective_id=1, has_side_effects=True, vmem_limit_bytes=56 * MIB
+            collective_id=1, has_side_effects=True, vmem_limit_bytes=60 * MIB
         ),
-    )(acts, score, w_gate, w_up)
+    )(acts, score, meta_all, cuts, w_gate, w_up)
     returned = lax.all_to_all(back, "expert", 0, 0, tiled=True)
-    own = width // slots
+
+    steps = slots // replicas
+
+    def from_slot(i):
+        return jnp.where(i == 0, steps - 1, i - 1)
+
     expert_grads = pl.pallas_call(
         lambda owners, *refs: weights_kernel(dims, owners, replicas, *refs),
         name="weight_grads",
         out_shape=jax.ShapeDtypeStruct((experts, 3, own, ff), BF),
         grid_spec=pltpu.PrefetchScalarGridSpec(
             num_scalar_prefetch=1,
-            grid=(slots,),
+            grid=(steps,),
             in_specs=[
-                pl.BlockSpec((per * slots, LANE), lambda i, o: (0, 0)),
-                pl.BlockSpec((2, per * slots, 2 * LANE), lambda i, o: (0, 0, 0)),
-                pl.BlockSpec(
-                    (1, rows, 3 * ff),
-                    lambda i, o: (jnp.where(i < replicas, experts + i, i - replicas), 0, 0),
-                ),
+                pl.BlockSpec((replicas, 2, own, rows), lambda i, o: (from_slot(i), 0, 0, 0)),
+                pl.BlockSpec((replicas, rows, 3 * ff), lambda i, o: (from_slot(i), 0, 0)),
             ],
             out_specs=pl.BlockSpec(
-                (1, 3, own, ff), lambda i, o: (jnp.maximum(i - replicas, 0), 0, 0, 0)
+                (replicas, 3, own, ff), lambda i, o: (jnp.maximum(i - 1, 0), 0, 0, 0)
             ),
-            scratch_shapes=[
-                pltpu.VMEM((RING, slots, line), F32),
-                pltpu.VMEM((RING, slots, line), F32),
-                pltpu.VMEM((rows, 2 * LANE), BF),
-                pltpu.VMEM((rows, 2 * LANE), BF),
-                pltpu.VMEM((replicas, 3, own, ff), F32),
-            ],
+            scratch_shapes=[pltpu.VMEM((replicas, 3, own, ff), F32)],
         ),
         compiler_params=pltpu.CompilerParams(vmem_limit_bytes=40 * MIB),
         cost_estimate=pl.CostEstimate(
-            flops=8_000_000_000, bytes_accessed=32_000_000, transcendentals=0
+            flops=5_000_000_000, bytes_accessed=40_000_000, transcendentals=0
         ),
-    )(replica_owner, meta_all, cuts, acts_all.reshape(slots, rows, 3 * ff))
+    )(replica_owner, turned_all, acts_all.reshape(slots, rows, 3 * ff))
     own_meta = jnp.concatenate([meta, jnp.full((LANE - per, LANE), -1, BF)], axis=0)
     input_grads, gate_grads = pl.pallas_call(
         functools.partial(tokens_kernel, dims),

time: 236 us -> 196 us (0.83)
  Pallas kernels: 226 us -> 177 us
  waiting for transfers between devices: 0.01 us -> 5.23 us
  local copies, waits for them, and re-layouts: 0.97 us -> 5.08 us
    pallas_call x1, Pallas kernels: 99.6 us -> 81.3 us  [per_device(): pl.pallas_call(functools.partial(dispatch_kernel, dims), name='dispatch',...]
    pallas_call x1, Pallas kernels: 33.5 us -> 17.5 us  [per_device(): pl.pallas_call(lambda owners, *refs: weights_kernel(dims, owners, replica...]
    pallas_call x1, Pallas kernels: 91.2 us -> 76.5 us  [per_device(): pl.pallas_call(functools.partial(return_kernel, dims), name='activations_...]
    all_to_all x1, waiting for transfers between devices: 0.01 us -> 5.23 us  [per_device(): returned = lax.all_to_all(back, 'expert', 0, 0, tiled=True)]
    unnamed x9 -> x7, local copies, waits for them, and re-layouts: 0.79 us -> 4.9 us
  transfers between devices with their start and end apart: 1 -> 1, of which waited for: 0 -> 1; matrix products, arithmetic and copies ran while one was open for 0% -> 0% of each run, Pallas kernels for 14% -> 9%
where the time goes in v1:
time: 196 us; the launch traced here: 195 us
  Pallas kernels  177 us (90%)
  starting transfers between devices  5.88 us (3%)
  waiting for transfers between devices  5.23 us (3%)
  local copies, waits for them, and re-layouts  5.08 us (3%)
    pallas_call x1, Pallas kernels, per_device(): pl.pallas_call(functools.partial(dispatch_kernel, dims), name='dispatch',...  81.3 us
    pallas_call x1, Pallas kernels, per_device(): pl.pallas_call(functools.partial(return_kernel, dims), name='activations_...  76.5 us
    pallas_call x1, Pallas kernels, per_device(): pl.pallas_call(lambda owners, *refs: weights_kernel(dims, owners, replica...  17.5 us
    all_to_all x1, starting transfers between devices, per_device(): returned = lax.all_to_all(back, 'expert', 0, 0, tiled=True)  5.88 us
    all_to_all x1, waiting for transfers between devices, per_device(): returned = lax.all_to_all(back, 'expert', 0, 0, tiled=True)  5.23 us
    unnamed x7, local copies, waits for them, and re-layouts  4.9 us
  transfers between devices with their start and end apart: 1, of which 1 were waited for; matrix products, arithmetic and copies ran while one was open for 0% of the time, Pallas kernels for 9%

profile of v1, /device:TPU:1, one launch (start us, length us, event | category | flops | bytes accessed | tf_op | source)
XLA Modules:
  0.0 195.5 jit_solution(3005966169505989430)
XLA Ops:
  0.6 0.7 convert_element_type.6
  1.3 0.1 copy.13
  1.4 0.8 copy.14
  2.2 0.1 pad.3.clone
  2.3 0.7 maximum_maximum_fusion.meta
  2.9 81.3 %dispatch.1 = (bf16[384,768]{1,0:T(8,128)(2,1)}, bf16[384,128]{1,0:T(8,128)(2,1)}, bf16[2,1024,256]{2,1,0:T(8,128)(2,1)}, bf16[1024,128]{1,0:T(8,128)(2,1)}) custom-call(bf16[32,7168]{1,0:T(8,128)(2,1)} %tokens.1, bf16[32,7168]{1,0:T(8,128)(2,1)} %cotangent.1, bf16[32,128]{1,0:T(8,128)(2,1)} %maximum_maximum_fusion.meta, bf16[7168,256]{1,0:T(8,128)(2,1)} %bitcast.8, ...), custom_call_target="tpu_custom_call" | custom-call | tf_op jit(solution)/shard_map/dispatch/pallas_call | solution.py:728
  84.2 76.5 %activations_out.1 = (bf16[4,4,2,384,768]{4,3,2,1,0:T(8,128)(2,1)}, bf16[32,2,224,384]{3,2,1,0:T(8,128)(2,1)}, bf16[32,16,1920]{2,1,0:T(8,128)(2,1)}) custom-call(bf16[384,768]{1,0:T(8,128)(2,1)} %get-tuple-element.12.acts, bf16[384,128]{1,0:T(8,128)(2,1)} %get-tuple-element.13.score, bf16[1024,128]{1,0:T(8,128)(2,1)} %get-tuple-element.14.meta_all, ...), custom_call_target="tpu_custom_call" | custom-call | tf_op jit(solution)/shard_map/activations_out/pallas_call | solution.py:760
  160.7 0.0 copy-start.2
  160.7 0.0 copy-start.1
  160.7 5.9 %all-to-all-start = ((bf16[32,16,1920]{2,1,0:T(8,128)(2,1)}), bf16[32,16,1920]{2,1,0:T(8,128)(2,1)S(1)}, u32[]{:S(2)}, u32[]{:S(2)}) async-start(bf16[32,16,1920]{2,1,0:T(8,128)(2,1)} %get-tuple-element.16), calls=%async_computation | async-start | bytes 3932160 | tf_op jit(solution)/shard_map/all_to_all | solution.py:795
  166.6 0.0 copy-done.2
  166.6 0.0 copy-done.1
  166.6 0.0 copy-start
  166.7 4.1 %copy-done = bf16[32,2,224,384]{3,2,1,0:T(8,128)(2,1)S(1)} copy-done((bf16[32,2,224,384]{3,2,1,0:T(8,128)(2,1)S(1)}, bf16[32,2,224,384]{3,2,1,0:T(8,128)(2,1)}, u32[]{:S(2)}) %copy-start) | copy-done | bytes 11010072
  170.8 17.5 %weight_grads.1 = bf16[28,3,224,256]{3,2,1,0:T(8,128)(2,1)} custom-call(s32[4]{0:T(128)S(1)} %copy-done.1, bf16[32,2,224,384]{3,2,1,0:T(8,128)(2,1)S(1)} %copy-done, bf16[32,384,768]{2,1,0:T(8,128)(2,1)} %bitcast.7), custom_call_target="tpu_custom_call" | custom-call | flops 5000000000 | bytes 40000000 | tf_op jit(solution)/shard_map/weight_grads/pallas_call | solution.py:802
  188.3 5.2 %all-to-all-done.back = bf16[32,16,1920]{2,1,0:T(8,128)(2,1)S(1)} async-done(((bf16[32,16,1920]{2,1,0:T(8,128)(2,1)}), bf16[32,16,1920]{2,1,0:T(8,128)(2,1)S(1)}, u32[]{:S(2)}, u32[]{:S(2)}) %all-to-all-start) | async-done | bytes 1966112 | tf_op jit(solution)/shard_map/all_to_all | solution.py:795
  193.5 1.4 token_grads.1
  194.9 0.6 convert_bitcast_fusion
  (2 shorter events, 0.0 us)
Async XLA Ops:
  160.7 5.9 %copy-start.2 = (bf16[32,128]{1,0:T(8,128)(2,1)S(1)}, bf16[32,128]{1,0:T(8,128)(2,1)}, u32[]{:S(2)}) copy-start(bf16[32,128]{1,0:T(8,128)(2,1)} %maximum_maximum_fusion.meta) | copy-start | bytes 24580
  160.7 5.9 %copy-start.1 = (s32[4]{0:T(128)S(1)}, s32[4]{0:T(128)}, u32[]{:S(2)}) copy-start(s32[4]{0:T(128)} %owners.1) | copy-start | bytes 52
  160.7 32.8 %all-to-all-start = ((bf16[32,16,1920]{2,1,0:T(8,128)(2,1)}), bf16[32,16,1920]{2,1,0:T(8,128)(2,1)S(1)}, u32[]{:S(2)}, u32[]{:S(2)}) async-start(bf16[32,16,1920]{2,1,0:T(8,128)(2,1)} %get-tuple-element.16), calls=%async_computation | async-start | bytes 3932160 | tf_op jit(solution)/shard_map/all_to_all | solution.py:795
  166.6 4.1 %copy-start = (bf16[32,2,224,384]{3,2,1,0:T(8,128)(2,1)S(1)}, bf16[32,2,224,384]{3,2,1,0:T(8,128)(2,1)}, u32[]{:S(2)}) copy-start(bf16[32,2,224,384]{3,2,1,0:T(8,128)(2,1)} %get-tuple-element.19.refs_0_) | copy-start | bytes 33030148

commit v2 on v1

--- a/solution.py
+++ b/solution.py
@@ -187,6 +187,56 @@
 
 
 ACROSS_COPIES = 5
+
+
+class RingSum:
+    def __init__(self, links, axis, at, far, sums, low, first, second):
+        self.l, self.axis, self.at, self.far, self.sums = links, axis, at, far, sums
+        self.me = getattr(links, axis)
+        self.high, self.down = up1(self.me), down1(self.me)
+        self.low, self.first, self.second = low, first, second
+
+    def to(self, v):
+        return self.l.to(**{self.axis: v})
+
+    def part(self, v, k):
+        if k == 0:
+            return self.at(v, self.low, self.first)
+        return self.at(v, self.low + self.first, self.second)
+
+    def sum_part(self, side, k):
+        low, count = (0, self.first) if k == 0 else (self.first, self.second)
+        return self.sums(side, low, count)
+
+    def one(self):
+        across, start = up1(self.high), self.l.start
+        high, down = self.to(self.high), self.to(self.down)
+        self.f0 = start(self.part(across, 0), self.far(0, self.first), high)
+        self.f1 = start(self.part(across, 1), self.far(1, self.second), down)
+        self.d0 = start(self.part(self.high, 1), self.sum_part(0, 1), high)
+        self.d1 = start(self.part(self.down, 0), self.sum_part(1, 0), down)
+
+    def two(self):
+        self.f0.wait_recv()
+        ref = self.part(self.high, 0)
+        ref[...] = (ref[...].astype(F32) + self.far(0, self.first)[...].astype(F32)).astype(BF)
+        self.s0 = self.l.start(ref, self.sum_part(0, 0), self.to(self.high))
+        self.f1.wait_recv()
+        ref = self.part(self.down, 1)
+        ref[...] = (ref[...].astype(F32) + self.far(1, self.second)[...].astype(F32)).astype(BF)
+        self.s1 = self.l.start(ref, self.sum_part(1, 1), self.to(self.down))
+
+    def three(self, put):
+        for copy in (self.d0, self.d1, self.s0, self.s1):
+            copy.wait_recv()
+        for k in range(2):
+            total = self.part(self.me, k)[...].astype(F32)
+            for side in range(2):
+                total = total + self.sum_part(side, k)[...].astype(F32)
+            put(0 if k == 0 else self.first, total.astype(BF))
+
+
+RING_COPIES = 6
 
 
 def entries(meta, slot, per, cap, top):
@@ -264,15 +314,14 @@
 
     quarter = SHARED * LANE
     straight = width - RING * quarter
-    half = straight // 2
 
     def across(first, gather):
         def ring(line):
             def at(owner, part=None):
                 low, count = {
                     None: (0, quarter),
-                    0: (0, quarter // 2),
-                    1: (quarter // 2, quarter // 2),
+                    0: (0, quarter // (2 * LANE) * LANE),
+                    1: (quarter // (2 * LANE) * LANE, quarter - quarter // (2 * LANE) * LANE),
                 }[part]
                 cols = pl.ds(pl.multiple_of(first + owner * quarter + low, LANE), count)
                 if gather.y_first:
@@ -292,10 +341,11 @@
     qa = piece(qx0 + t * quarter, quarter, True, False)
     qb = piece(qdy0 + t * quarter, quarter, False, False)
     xa, xb = across(qx0, qa), across(qdy0, qb)
+    half = straight // (2 * LANE) * LANE
     p0 = piece(0, x0 + half, True)
-    p1 = piece(x0 + half, half, False)
+    p1 = piece(x0 + half, straight - half, False)
     p2 = piece(dy0, half, True)
-    p3 = piece(dy0 + half, half, False)
+    p3 = piece(dy0 + half, straight - half, False)
     qa.one()
     qb.one()
     qa.two()
@@ -456,9 +506,10 @@
 def return_kernel(
     dims,
     acts, score, meta_all, cuts, w_gate, w_up,
-    acts_all, turned_all, back,
-    held_all, wg, wu, a, far, up_buf, down_buf, far_in, sum_in, own_buf, score_in,
-    row_at, gate_at, rows_buf, turned,
+    slot_grads, input_grads, gate_grads,
+    held_all, wg, wu, far, up_buf, down_buf, far_in, sum_in, score_in,
+    row_at, gate_at, rows_buf, turned, by_token, block_sum,
+    y_far, y_sums, y_total, z_far, z_sums, z_total, stage,
     send, recv, local, out_sem,
 ):
     per, width, cap, top, ff = dims
@@ -468,13 +519,14 @@
     half = part // 2
     links = Links(send, recv)
     y, z, c, t = links.y, links.z, links.c, links.t
+    a = acts
+    me = lax.axis_index("expert")
     own = pltpu.make_async_copy(acts, held_all.at[y, z, c], local.at[0])
-    held = pltpu.make_async_copy(acts, a, local.at[1])
     weights = [
         pltpu.make_async_copy(w_gate, wg, local.at[2]),
         pltpu.make_async_copy(w_up, wu, local.at[3]),
     ]
-    for copy in [own, held] + weights:
+    for copy in [own] + weights:
         copy.start()
     own.wait()
     right, left, across = links.to(t=up1(t)), links.to(t=down1(t)), links.to(t=up1(up1(t)))
@@ -489,18 +541,6 @@
             return held_all.at[yy, zz, c, pl.ds(low, high - low), :]
 
         return Gather(links, at, y_first)
-
-    outs = []
-
-    def copy_out(gather, index, core):
-        line = gather.lines()[index]
-        r = pl.ds(0, rows // 2) if gather.y_first else pl.ds(rows // 2, rows // 2)
-        if gather.y_first:
-            src, dst = held_all.at[:, line, core, r, :], acts_all.at[:, line, core, r, :]
-        else:
-            src, dst = held_all.at[line, :, core, r, :], acts_all.at[line, :, core, r, :]
-        outs.append(pltpu.make_async_copy(src, dst, out_sem.at[len(outs)]))
-        outs[-1].start()
 
     group_rows = rows // RING
     line_tokens = per * slots // RING
@@ -541,163 +581,279 @@
     g1 = piece(rows // 2, rows, False)
     g0.one()
     g1.one()
-    held.wait()
     for copy in weights:
         copy.wait()
 
-    def term(quarter, column):
-        r = pl.ds(pl.multiple_of(quarter * part + column, LANE), LANE)
-        return dot(a[:, 0:ff], wg[r, :], NT) + dot(a[:, ff : 2 * ff], wu[r, :], NT)
-
-    def fill(out, quarter, low, high, extra=None):
-        def step(i, carry):
-            column = pl.multiple_of(low + i * LANE, LANE)
-            total = term(quarter, column)
-            if extra is not None:
-                total = total + extra(column)
-            out[:, pl.ds(column, LANE)] = total.astype(BF)
-            return carry
-
-        lax.fori_loop(0, (high - low) // LANE, step, 0)
-
-    first, second = pl.ds(0, half), pl.ds(half, half)
-    fill(far, up1(up1(t)), 0, part)
-    f_right = links.start(far.at[:, first], far_in.at[:, first], right)
-    f_left = links.start(far.at[:, second], far_in.at[:, second], left)
+    def fill(out, quarter, low, count, extra=None):
+        r = pl.ds(pl.multiple_of(quarter * part + low, LANE), count)
+        sums = dot(a[:, 0:ff], wg[r, :], NT) + dot(a[:, ff : 2 * ff], wu[r, :], NT)
+        for more in extra or ():
+            sums = sums + more[...].astype(F32)
+        out[:, pl.ds(low, count)] = sums.astype(BF)
+
+    pieces = []
+    for low in (0, half):
+        first = half // (2 * LANE) * LANE + LANE
+        pieces.append(((low, first), (low + first, half - first)))
+
+    def cols_of(span):
+        return pl.ds(*span)
+
+    far_copies, straight, summed = [], [], []
+
+    def send_far(h):
+        one, two = pieces[h]
+        fill(far, up1(up1(t)), h * half, half)
+        far_copies.append(
+            (
+                links.start(far.at[:, cols_of(one)], far_in.at[:, cols_of(one)], right),
+                links.start(far.at[:, cols_of(two)], far_in.at[:, cols_of(two)], left),
+            )
+        )
+
+    def send_straight(h):
+        one, two = pieces[h]
+        fill(up_buf, up1(t), *two)
+        d_right = links.start(
+            up_buf.at[:, cols_of(two)], sum_in.at[0, :, cols_of(two)], right
+        )
+        fill(down_buf, down1(t), *one)
+        d_left = links.start(
+            down_buf.at[:, cols_of(one)], sum_in.at[1, :, cols_of(one)], left
+        )
+        straight.append((d_right, d_left))
+
+    def send_summed(h):
+        one, two = pieces[h]
+        f_right, f_left = far_copies[h]
+        f_right.wait_recv()
+        fill(up_buf, up1(t), *one, [far_in.at[:, cols_of(one)]])
+        s_right = links.start(
+            up_buf.at[:, cols_of(one)], sum_in.at[0, :, cols_of(one)], right
+        )
+        f_left.wait_recv()
+        fill(down_buf, down1(t), *two, [far_in.at[:, cols_of(two)]])
+        s_left = links.start(
+            down_buf.at[:, cols_of(two)], sum_in.at[1, :, cols_of(two)], left
+        )
+        summed.append((s_right, s_left))
+
+    wide = part + LANE
+    shared, chosen_rows = [], []
+
+    def to_tokens(h, score_rows=None):
+        for copy in (*straight[h], *summed[h]):
+            copy.wait_recv()
+        cols = pl.ds(h * half, half)
+        fill(far_in, t, h * half, half, [sum_in.at[0, :, cols], sum_in.at[1, :, cols]])
+        low, stop = h * half, half if h == 0 else wide
+        for g in range(RING):
+            chosen = picks(row_at[g, pl.ds(me, 1), :], group_rows).astype(BF)
+            r = pl.ds(g * group_rows, group_rows)
+            found = dot(chosen, far_in[r, cols], TN).astype(BF)
+            by_token[g, :, :, :, cols] = found.reshape(RING, CORES, per, half)
+            if h == 1:
+                named = meta_all[pl.ds(g * line_tokens, line_tokens), :].astype(F32)
+                lanes = lax.broadcasted_iota(jnp.int32, (line_tokens, LANE), 1)
+                found = dot(
+                    chosen, score_rows[g * group_rows : (g + 1) * group_rows], TN
+                )
+                found = jnp.where((named == me.astype(F32)) & (lanes < top), found, 0.0)
+                by_token[g, :, :, :, pl.ds(part, LANE)] = found.astype(BF).reshape(
+                    RING, CORES, per, LANE
+                )
+        cols = pl.ds(low, stop - low)
+        shared.append(
+            links.start(
+                by_token.at[:, :, 1 - c, :, cols], block_sum.at[:, :, :, cols], links.to(c=1 - c)
+            )
+        )
+
+    def add_core(h):
+        shared[h].wait_recv()
+        low, stop = h * half, half if h == 0 else wide
+        cols = pl.ds(low, stop - low)
+        for g in range(RING):
+            mine = by_token[g, :, pl.ds(c, 1), :, cols].reshape(RING, per, stop - low)
+            block_sum[g, :, :, cols] = (
+                block_sum[g, :, :, cols].astype(F32) + mine.astype(F32)
+            ).astype(BF)
+
+    rest = (wide - half) // 2
+    spans = (
+        (0, pieces[0][0][1], pieces[0][1][1]),
+        (half, rest // 2, rest // 2),
+        (half + rest, rest // 2, rest // 2),
+    )
+    firsts, seconds = [], []
+
+    def ring_one(k):
+        y_first = k < 2
+
+        def at(v, lo, count):
+            if y_first:
+                return block_sum.at[v, :, :, pl.ds(lo, count)]
+            return block_sum.at[:, v, :, pl.ds(lo, count)]
+
+        firsts.append(
+            RingSum(
+                links,
+                "y" if y_first else "z",
+                at,
+                lambda side, count: y_far.at[k, side, :, :, pl.ds(0, count)],
+                lambda side, lo, count: y_sums.at[k, side, :, :, pl.ds(lo, count)],
+                *spans[k],
+            )
+        )
+        firsts[k].one()
+
+    def ring_two(k):
+        def put(lo, value):
+            y_total[k, :, :, pl.ds(lo, value.shape[-1])] = value
+
+        firsts[k].three(put)
+        seconds.append(
+            RingSum(
+                links,
+                "z" if k < 2 else "y",
+                lambda v, lo, count: y_total.at[k, v, :, pl.ds(lo, count)],
+                lambda side, count: z_far.at[k, side, :, pl.ds(0, count)],
+                lambda side, lo, count: z_sums.at[k, side, :, pl.ds(lo, count)],
+                0,
+                *spans[k][1:],
+            )
+        )
+        seconds[k].one()
+
+    def ring_end(k):
+        def put(lo, value):
+            z_total[:, pl.ds(spans[k][0] + lo, value.shape[-1])] = value
+
+        seconds[k].three(put)
+
+    send_far(0)
+    send_far(1)
     g0.two()
     g1.two()
-    fill(up_buf, up1(t), half, part)
-    d_right = links.start(up_buf.at[:, second], sum_in.at[0, :, second], right)
-    fill(down_buf, down1(t), 0, half)
-    d_left = links.start(down_buf.at[:, first], sum_in.at[1, :, first], left)
+    send_straight(0)
+    place_rows()
+    g0.three()
+    g1.three()
+    send_summed(0)
+    send_straight(1)
     scores = [
         links.start(score, score_in.at[0], right),
         links.start(score, score_in.at[1], left),
         links.start(score, score_in.at[2], across),
     ]
-    place_rows()
-    g0.three()
-    g1.three()
-    copy_out(g0, 0, c)
-    copy_out(g1, 0, c)
-    f_right.wait_recv()
-    fill(up_buf, up1(t), 0, half, lambda k: far_in[:, pl.ds(k, LANE)].astype(F32))
-    s_right = links.start(up_buf.at[:, first], sum_in.at[0, :, first], right)
-    f_left.wait_recv()
-    fill(down_buf, down1(t), half, part, lambda k: far_in[:, pl.ds(k, LANE)].astype(F32))
-    s_left = links.start(down_buf.at[:, second], sum_in.at[1, :, second], left)
-    lax.fori_loop(0, slots // several, turn_step, 0)
-    turned_out = pltpu.make_async_copy(turned, turned_all, local.at[4])
-    turned_out.start()
+    lax.fori_loop(0, slots // several // 2, turn_step, 0)
+    send_summed(1)
+    lax.fori_loop(slots // several // 2, slots // several, turn_step, 0)
     g0.four()
     g1.four()
-    for gather in (g0, g1):
-        copy_out(gather, 1, c)
-        copy_out(gather, 2, c)
+    to_tokens(0)
+    add_core(0)
+    ring_one(0)
     for copy in scores:
         copy.wait_recv()
     total = jnp.zeros((rows, 1), F32)
     for ref in (score, score_in.at[0], score_in.at[1], score_in.at[2]):
         both = ref[...].astype(F32)
         total = total + (both[:, 0:1] + both[:, LANE // 2 : LANE // 2 + 1])
-    padded = 16
-    spread = jnp.where(
-        (
-            lax.div(lax.broadcasted_iota(jnp.int32, (slots * padded, rows), 0), padded) * cap
-            + lax.rem(lax.broadcasted_iota(jnp.int32, (slots * padded, rows), 0), padded)
-            == lax.broadcasted_iota(jnp.int32, (slots * padded, rows), 1)
-        )
-        & (
-            lax.rem(lax.broadcasted_iota(jnp.int32, (slots * padded, rows), 0), padded) < cap
-        ),
-        1.0,
-        0.0,
-    ).astype(BF)
-    back[:, :, pl.ds(part, LANE)] = (
-        dot(spread, jnp.broadcast_to(total, (rows, LANE)).astype(BF))
-        .astype(BF)
-        .reshape(slots, padded, LANE)
-    )
-    for copy in (d_right, d_left, s_right, s_left):
-        copy.wait_recv()
-
-    def last(i, carry):
-        column = pl.multiple_of(i * LANE, LANE)
-        cols = pl.ds(column, LANE)
-        total = term(t, column) + sum_in[0, :, cols].astype(F32) + sum_in[1, :, cols].astype(F32)
-        own_buf[...] = total.astype(BF)
-        back[:, :, cols] = dot(spread, own_buf[...]).astype(BF).reshape(slots, padded, LANE)
-        return carry
-
-    lax.fori_loop(0, part // LANE, last, 0)
+    score_rows = jnp.broadcast_to(total, (rows, LANE)).astype(BF)
     g0.five()
     g1.five()
-    for gather in (g0, g1):
-        copy_out(gather, 3, c)
+    firsts[0].two()
+    to_tokens(1, score_rows)
+    ring_two(0)
     for gather in (g0, g1):
         gather.six()
-        for index in range(RING):
-            copy_out(gather, index, 1 - c)
+
+    stored = []
+
+    def grads(i):
+        slot = i % 2
+        if i >= 2:
+            stored[i - 2].wait()
+
+        def step(j, carry):
+            place = (i // 2, (i % 2) * 2 + lax.div(j, CORES), lax.rem(j, CORES))
+            own_slot = i * several + j
+            both = dot(turned[own_slot, 0], held_all[(*place, slice(None), pl.ds(0, 2 * ff))])
+            stage[slot, j, 0] = both[:, :ff].astype(BF)
+            stage[slot, j, 1] = both[:, ff:].astype(BF)
+            stage[slot, j, 2] = dot(
+                turned[own_slot, 1], held_all[(*place, slice(None), pl.ds(2 * ff, ff))]
+            ).astype(BF)
+            return carry
+
+        lax.fori_loop(0, several, step, 0)
+        stored.append(
+            pltpu.make_async_copy(
+                stage.at[slot],
+                slot_grads.at[pl.ds(i * several, several)],
+                out_sem.at[i],
+            )
+        )
+        stored[-1].start()
+
+    add_core(1)
+    ring_one(1)
+    ring_one(2)
+    seconds[0].two()
+    grads(0)
+    firsts[1].two()
+    firsts[2].two()
+    grads(1)
+    grads(2)
+    ring_two(1)
+    ring_two(2)
+    grads(3)
+    seconds[1].two()
+    seconds[2].two()
+    grads(4)
+    grads(5)
+    for k in range(3):
+        ring_end(k)
+    input_grads[...] = z_total[:, pl.ds(0, part)]
+    gate_grads[...] = z_total[:, pl.ds(part, LANE)]
+    grads(6)
+    grads(7)
     links.drain()
-    turned_out.wait()
-    for copy in outs:
-        copy.wait()
-
-
-def weights_kernel(dims, owners, replicas, turned, acts, out, kept):
-    ff = dims[-1]
-    i = pl.program_id(0)
-
-    def parts(j):
-        in_grads = dot(turned[j, 0], acts[j, :, 0 : 2 * ff])
-        down = dot(turned[j, 1], acts[j, :, 2 * ff :])
-        return in_grads[:, :ff], in_grads[:, ff:], down
-
-    @pl.when(i == 0)
-    def _():
-        for j in range(replicas):
-            for k, part in enumerate(parts(j)):
-                kept[j, k] = part
-
-    @pl.when(i > 0)
-    def _():
-        for j in range(replicas):
-            for k, part in enumerate(parts(j)):
-                out[j, k] = part.astype(BF)
-            expert = (i - 1) * replicas + j
-            owned = owners[0] == expert
-            for r in range(1, replicas):
-                owned = owned | (owners[r] == expert)
-
-            @pl.when(owned)
-            def _():
-                for k in range(3):
-                    total = out[j, k].astype(F32)
-                    for r in range(replicas):
-                        total = total + jnp.where(owners[r] == expert, kept[r, k], 0.0)
-                    out[j, k] = total.astype(BF)
-
-
-def tokens_kernel(dims, meta, back, input_grads, gate_grads):
-    per, width, cap, top, ff = dims
-    slots = RING * RING * CORES
-    part = width // RING
-    padded = back.shape[1]
-    ids = lax.broadcasted_iota(jnp.int32, (slots, 1), 0)
-    row, _, turned = entries(meta[...], ids, per, cap, top)
-    place = lax.broadcasted_iota(jnp.int32, (slots, padded, LANE), 1).astype(F32)
-    chosen = jnp.where(row[:, None, :] == place, 1.0, 0.0)
-    flat = chosen.reshape(slots * padded, LANE).astype(BF)
-    for k in range(part // (2 * LANE)):
-        cols = pl.ds(k * 2 * LANE, 2 * LANE)
-        rows = back[:, :, cols].reshape(slots * padded, 2 * LANE)
-        input_grads[:, cols] = dot(flat, rows, TN)[:per].astype(BF)
-    score = back[:, :, pl.ds(part, LANE)].astype(F32)
-    by_slot = jnp.sum(chosen * score, axis=1)
-    for k in range(top):
-        same = turned[k : k + 1] == ids.astype(F32)
-        line = jnp.sum(jnp.where(same, by_slot, 0.0), axis=0, keepdims=True)
-        gate_grads[pl.ds(k, 1), :] = line[:, :per]
+    stored[-2].wait()
+    stored[-1].wait()
+
+
+def combine_kernel(replicas, owners, slot_grads, out, copies, held, sems):
+    experts = out.shape[0]
+    load = pltpu.make_async_copy(
+        slot_grads.at[pl.ds(experts, replicas)], copies, sems.at[2 * experts]
+    )
+    load.start()
+    loads, stores = [], []
+    for e in range(experts):
+        loads.append(pltpu.make_async_copy(slot_grads.at[e], held.at[e], sems.at[e]))
+        stores.append(pltpu.make_async_copy(held.at[e], out.at[e], sems.at[experts + e]))
+        loads[e].start()
+    load.wait()
+    for e in range(experts):
+        loads[e].wait()
+        owned = owners[0] == e
+        for r in range(1, replicas):
+            owned = owned | (owners[r] == e)
+
+        @pl.when(owned)
+        def _():
+            for k in range(3):
+                total = held[e, k].astype(F32)
+                for r in range(replicas):
+                    same = jnp.where(owners[r] == e, 1.0, 0.0)
+                    total = total + same * copies[r, k].astype(F32)
+                held[e, k] = total.astype(BF)
+
+        stores[e].start()
+    for store in stores:
+        store.wait()
 
 
 def per_device(tokens, cotangent, gate_weights, route_slots, replica_owner, w_gate, w_up, w_down):
@@ -755,88 +911,67 @@
             collective_id=0, has_side_effects=True, vmem_limit_bytes=56 * MIB
         ),
     )(tokens, cotangent, meta, w_gate, w_up, w_down)
-    copies = 2 * GATHER_COPIES + 9
+    copies = 2 * GATHER_COPIES + 15 + 2 + 6 * RING_COPIES
     own = width // slots
-    acts_all, turned_all, back = pl.pallas_call(
+    wide = part + LANE
+    half = part // 2
+    piece = half // (2 * LANE) * LANE + LANE
+    slot_grads, input_grads, gate_grads = pl.pallas_call(
         functools.partial(return_kernel, dims),
-        name="activations_out",
+        name="grads_back",
         out_shape=(
-            jax.ShapeDtypeStruct((RING, RING, CORES, rows, 3 * ff), BF),
-            jax.ShapeDtypeStruct((slots, 2, own, rows), BF),
-            jax.ShapeDtypeStruct((slots, padded, part + LANE), BF),
+            jax.ShapeDtypeStruct((slots, 3, own, ff), BF),
+            jax.ShapeDtypeStruct((per, part), BF),
+            jax.ShapeDtypeStruct((per, LANE), BF),
         ),
-        in_specs=[any_, vmem, vmem, vmem, any_, any_],
-        out_specs=(any_, any_, vmem),
+        in_specs=[vmem, vmem, vmem, vmem, any_, any_],
+        out_specs=(any_, vmem, vmem),
         scratch_shapes=[
             pltpu.VMEM((RING, RING, CORES, rows, 3 * ff), BF),
             pltpu.VMEM((width, ff), BF),
             pltpu.VMEM((width, ff), BF),
-            pltpu.VMEM((rows, 3 * ff), BF),
             pltpu.VMEM((rows, part), BF),
             pltpu.VMEM((rows, part), BF),
             pltpu.VMEM((rows, part), BF),
             pltpu.VMEM((rows, part), BF),
             pltpu.VMEM((2, rows, part), BF),
-            pltpu.VMEM((rows, LANE), BF),
             pltpu.VMEM((3, rows, LANE), BF),
             pltpu.VMEM((RING, slots, line), F32),
             pltpu.VMEM((RING, slots, line), F32),
             pltpu.VMEM((4, 2, rows, 2 * LANE), BF),
             pltpu.VMEM((slots, 2, own, rows), BF),
+            pltpu.VMEM((RING, RING, CORES, per, wide), BF),
+            pltpu.VMEM((RING, RING, per, wide), BF),
+            pltpu.VMEM((3, 2, RING, per, piece), BF),
+            pltpu.VMEM((3, 2, RING, per, half), BF),
+            pltpu.VMEM((3, RING, per, half), BF),
+            pltpu.VMEM((3, 2, per, piece), BF),
+            pltpu.VMEM((3, 2, per, half), BF),
+            pltpu.VMEM((per, wide), BF),
+            pltpu.VMEM((2, 4, 3, own, ff), BF),
             pltpu.SemaphoreType.DMA((copies,)),
             pltpu.SemaphoreType.DMA((copies,)),
-            pltpu.SemaphoreType.DMA((5,)),
-            pltpu.SemaphoreType.DMA((4 * RING,)),
+            pltpu.SemaphoreType.DMA((4,)),
+            pltpu.SemaphoreType.DMA((slots // 4,)),
         ],
         compiler_params=pltpu.CompilerParams(
-            collective_id=1, has_side_effects=True, vmem_limit_bytes=60 * MIB
+            collective_id=1, has_side_effects=True, vmem_limit_bytes=62 * MIB
         ),
     )(acts, score, meta_all, cuts, w_gate, w_up)
-    returned = lax.all_to_all(back, "expert", 0, 0, tiled=True)
-
-    steps = slots // replicas
-
-    def from_slot(i):
-        return jnp.where(i == 0, steps - 1, i - 1)
-
     expert_grads = pl.pallas_call(
-        lambda owners, *refs: weights_kernel(dims, owners, replicas, *refs),
-        name="weight_grads",
+        functools.partial(combine_kernel, replicas),
+        name="combine",
         out_shape=jax.ShapeDtypeStruct((experts, 3, own, ff), BF),
-        grid_spec=pltpu.PrefetchScalarGridSpec(
-            num_scalar_prefetch=1,
-            grid=(steps,),
-            in_specs=[
-                pl.BlockSpec((replicas, 2, own, rows), lambda i, o: (from_slot(i), 0, 0, 0)),
-                pl.BlockSpec((replicas, rows, 3 * ff), lambda i, o: (from_slot(i), 0, 0)),
-            ],
-            out_specs=pl.BlockSpec(
-                (replicas, 3, own, ff), lambda i, o: (jnp.maximum(i - 1, 0), 0, 0, 0)
-            ),
-            scratch_shapes=[pltpu.VMEM((replicas, 3, own, ff), F32)],
-        ),
-        compiler_params=pltpu.CompilerParams(vmem_limit_bytes=40 * MIB),
-        cost_estimate=pl.CostEstimate(
-            flops=5_000_000_000, bytes_accessed=40_000_000, transcendentals=0
-        ),
-    )(replica_owner, turned_all, acts_all.reshape(slots, rows, 3 * ff))
-    own_meta = jnp.concatenate([meta, jnp.full((LANE - per, LANE), -1, BF)], axis=0)
-    input_grads, gate_grads = pl.pallas_call(
-        functools.partial(tokens_kernel, dims),
-        name="token_grads",
-        out_shape=(
-            jax.ShapeDtypeStruct((per, part), BF),
-            jax.ShapeDtypeStruct((top, per), F32),
-        ),
-        in_specs=[vmem, vmem],
-        out_specs=(vmem, vmem),
-        compiler_params=pltpu.CompilerParams(vmem_limit_bytes=32 * MIB),
-    )(own_meta, returned)
-    return (
-        input_grads,
-        jnp.transpose(gate_grads.astype(BF)),
-        jnp.transpose(expert_grads, (0, 2, 1, 3)),
-    )
+        in_specs=[pl.BlockSpec(memory_space=pltpu.SMEM), any_],
+        out_specs=any_,
+        scratch_shapes=[
+            pltpu.VMEM((replicas, 3, own, ff), BF),
+            pltpu.VMEM((experts, 3, own, ff), BF),
+            pltpu.SemaphoreType.DMA((2 * experts + 1,)),
+        ],
+        compiler_params=pltpu.CompilerParams(vmem_limit_bytes=60 * MIB),
+    )(replica_owner, slot_grads)
+    return input_grads, gate_grads[:, :top], jnp.transpose(expert_grads, (0, 2, 1, 3))
 
 
 def solution(mesh):

time: 196 us -> 182 us (0.929)
  starting transfers between devices: 5.88 us -> 0 us
  waiting for transfers between devices: 5.23 us -> 0 us
  local copies, waits for them, and re-layouts: 5.08 us -> 2.93 us
  Pallas kernels: 177 us -> 175 us
    all_to_all x1 -> x0, starting transfers between devices: 5.88 us -> none  [per_device(): returned = lax.all_to_all(back, 'expert', 0, 0, tiled=True)]
    all_to_all x1 -> x0, waiting for transfers between devices: 5.23 us -> none  [per_device(): returned = lax.all_to_all(back, 'expert', 0, 0, tiled=True)]
    unnamed x7 -> x5, local copies, waits for them, and re-layouts: 4.9 us -> 2.76 us
    pallas_call x3 -> x2, Pallas kernels: 95.3 us -> 93.4 us  [the longest x1 84.4 us: per_device(): pl.pallas_call(functools.partial(return_kernel, dims), name='grads_back',...]
  transfers between devices with their start and end apart: 1 -> 0, of which waited for: 1 -> 0; matrix products, arithmetic and copies ran while one was open for 0% -> 0% of each run, Pallas kernels for 9% -> 0%
where the time goes in v2:
time: 182 us; the launch traced here: 180 us
  Pallas kernels  175 us (96%)
  local copies, waits for them, and re-layouts  2.93 us (2%)
    pallas_call x1, Pallas kernels, per_device(): pl.pallas_call(functools.partial(return_kernel, dims), name='grads_back',...  84.4 us
    pallas_call x1, Pallas kernels, per_device(): pl.pallas_call(functools.partial(dispatch_kernel, dims), name='dispatch',...  81.4 us
    pallas_call x1, Pallas kernels, per_device(): pl.pallas_call(functools.partial(combine_kernel, replicas), name='combine...  9.05 us

profile of v2, /device:TPU:1, one launch (start us, length us, event | category | flops | bytes accessed | tf_op | source)
XLA Modules:
  0.0 179.8 jit_solution(5405719029458434445)
XLA Ops:
  0.6 0.1 pad.2.clone
  0.7 0.7 convert_element_type.3
  1.4 0.1 copy.14
  1.5 0.8 copy.15
  2.3 0.7 maximum_maximum_fusion.meta
  2.9 81.4 %dispatch.1 = (bf16[384,768]{1,0:T(8,128)(2,1)}, bf16[384,128]{1,0:T(8,128)(2,1)}, bf16[2,1024,256]{2,1,0:T(8,128)(2,1)}, bf16[1024,128]{1,0:T(8,128)(2,1)}) custom-call(bf16[32,7168]{1,0:T(8,128)(2,1)} %tokens.1, bf16[32,7168]{1,0:T(8,128)(2,1)} %cotangent.1, bf16[32,128]{1,0:T(8,128)(2,1)} %maximum_maximum_fusion.meta, bf16[7168,256]{1,0:T(8,128)(2,1)} %bitcast.5, ...), custom_call_target="tpu_custom_call" | custom-call | tf_op jit(solution)/shard_map/dispatch/pallas_call | solution.py:884
  84.3 84.4 %grads_back.1 = (bf16[32,3,224,256]{3,2,1,0:T(8,128)(2,1)}, bf16[32,1792]{1,0:T(8,128)(2,1)}, bf16[32,128]{1,0:T(8,128)(2,1)}) custom-call(bf16[384,768]{1,0:T(8,128)(2,1)} %get-tuple-element.10.acts, bf16[384,128]{1,0:T(8,128)(2,1)} %get-tuple-element.11.score, bf16[1024,128]{1,0:T(8,128)(2,1)} %get-tuple-element.12.meta_all, ...), custom_call_target="tpu_custom_call" | custom-call | tf_op jit(solution)/shard_map/grads_back/pallas_call | solution.py:919
  168.7 1.3 copy.16
  170.0 0.0 copy-start
  170.0 9.1 %combine.1 = bf16[28,3,224,256]{3,2,1,0:T(8,128)(2,1)} custom-call(s32[4]{0:T(128)} %owners.1, bf16[32,3,224,256]{3,2,1,0:T(8,128)(2,1)} %get-tuple-element.16.slot_grads), custom_call_target="tpu_custom_call" | custom-call | tf_op jit(solution)/shard_map/combine/pallas_call | solution.py:961
  179.1 0.0 copy-done
  179.1 0.6 copy.18
  (1 shorter events, 0.0 us)
Async XLA Ops:
  170.0 9.1 %copy-start = (bf16[32,1792]{1,0:T(8,128)(2,1)S(1)}, bf16[32,1792]{1,0:T(8,128)(2,1)}, u32[]{:S(2)}) copy-start(bf16[32,1792]{1,0:T(8,128)(2,1)} %get-tuple-element.26) | copy-start | bytes 344068

commit v3 on v2

--- a/solution.py
+++ b/solution.py
@@ -12,6 +12,7 @@
 F32 = jnp.float32
 LANE = 128
 SHARED = 6
+CHUNK = 1024
 RING = 4
 CORES = 2
 MIB = 1 << 20
@@ -406,7 +407,7 @@
             jnp.sum(chosen * gate[0:1], axis=1, keepdims=True), (group_rows, LANE)
         )
 
-    chunk = 512
+    chunk = CHUNK
 
     def fill_rows(start):
         for g in range(RING):
@@ -797,27 +798,27 @@
         )
         stored[-1].start()
 
+    grads(0)
     add_core(1)
     ring_one(1)
     ring_one(2)
     seconds[0].two()
-    grads(0)
+    grads(1)
+    grads(2)
     firsts[1].two()
     firsts[2].two()
-    grads(1)
-    grads(2)
+    grads(3)
+    grads(4)
     ring_two(1)
     ring_two(2)
-    grads(3)
+    grads(5)
     seconds[1].two()
     seconds[2].two()
-    grads(4)
-    grads(5)
+    grads(6)
     for k in range(3):
         ring_end(k)
     input_grads[...] = z_total[:, pl.ds(0, part)]
     gate_grads[...] = z_total[:, pl.ds(part, LANE)]
-    grads(6)
     grads(7)
     links.drain()
     stored[-2].wait()
@@ -897,7 +898,7 @@
             pltpu.VMEM((width, ff), BF),
             pltpu.VMEM((width, ff), BF),
             pltpu.VMEM((width, ff), BF),
-            pltpu.VMEM((rows, 512), BF),
+            pltpu.VMEM((rows, CHUNK), BF),
             pltpu.VMEM((rows, ff), F32),
             pltpu.VMEM((rows, ff), F32),
             pltpu.VMEM((rows, ff), F32),

time: 182 us -> 180 us (0.989)
  Pallas kernels: 175 us -> 171 us
where the time goes in v3:
time: 180 us; the launch traced here: 176 us
  Pallas kernels  171 us (95%)
  local copies, waits for them, and re-layouts  2.93 us (2%)
    pallas_call x1, Pallas kernels, per_device(): pl.pallas_call(functools.partial(return_kernel, dims), name='grads_back',...  82.6 us
    pallas_call x1, Pallas kernels, per_device(): pl.pallas_call(functools.partial(dispatch_kernel, dims), name='dispatch',...  79.8 us
    pallas_call x1, Pallas kernels, per_device(): pl.pallas_call(functools.partial(combine_kernel, replicas), name='combine...  8.93 us

profile of v3, /device:TPU:1, one launch (start us, length us, event | category | flops | bytes accessed | tf_op | source)
XLA Modules:
  0.0 176.3 jit_solution(15604981663328776540)
XLA Ops:
  0.6 0.1 pad.2.clone
  0.7 0.7 convert_element_type.3
  1.4 0.1 copy.14
  1.5 0.8 copy.15
  2.3 0.7 maximum_maximum_fusion.meta
  2.9 79.8 %dispatch.1 = (bf16[384,768]{1,0:T(8,128)(2,1)}, bf16[384,128]{1,0:T(8,128)(2,1)}, bf16[2,1024,256]{2,1,0:T(8,128)(2,1)}, bf16[1024,128]{1,0:T(8,128)(2,1)}) custom-call(bf16[32,7168]{1,0:T(8,128)(2,1)} %tokens.1, bf16[32,7168]{1,0:T(8,128)(2,1)} %cotangent.1, bf16[32,128]{1,0:T(8,128)(2,1)} %maximum_maximum_fusion.meta, bf16[7168,256]{1,0:T(8,128)(2,1)} %bitcast.5, ...), custom_call_target="tpu_custom_call" | custom-call | tf_op jit(solution)/shard_map/dispatch/pallas_call | solution.py:885
  82.7 82.6 %grads_back.1 = (bf16[32,3,224,256]{3,2,1,0:T(8,128)(2,1)}, bf16[32,1792]{1,0:T(8,128)(2,1)}, bf16[32,128]{1,0:T(8,128)(2,1)}) custom-call(bf16[384,768]{1,0:T(8,128)(2,1)} %get-tuple-element.10.acts, bf16[384,128]{1,0:T(8,128)(2,1)} %get-tuple-element.11.score, bf16[1024,128]{1,0:T(8,128)(2,1)} %get-tuple-element.12.meta_all, ...), custom_call_target="tpu_custom_call" | custom-call | tf_op jit(solution)/shard_map/grads_back/pallas_call | solution.py:920
  165.3 1.3 copy.16
  166.7 0.0 copy-start
  166.7 8.9 %combine.1 = bf16[28,3,224,256]{3,2,1,0:T(8,128)(2,1)} custom-call(s32[4]{0:T(128)} %owners.1, bf16[32,3,224,256]{3,2,1,0:T(8,128)(2,1)} %get-tuple-element.16.slot_grads), custom_call_target="tpu_custom_call" | custom-call | tf_op jit(solution)/shard_map/combine/pallas_call | solution.py:962
  175.6 0.0 copy-done
  175.6 0.6 copy.18
  (1 shorter events, 0.0 us)
Async XLA Ops:
  166.7 8.9 %copy-start = (bf16[32,1792]{1,0:T(8,128)(2,1)S(1)}, bf16[32,1792]{1,0:T(8,128)(2,1)}, u32[]{:S(2)}) copy-start(bf16[32,1792]{1,0:T(8,128)(2,1)} %get-tuple-element.26) | copy-start | bytes 344068

commit v4 on v3

--- a/solution.py
+++ b/solution.py
@@ -493,12 +493,12 @@
     p2.five()
     p3.five()
     xb[3].three()
+    for ring in xb:
+        ring.four()
+    lax.fori_loop(plain, steps, dy_step, 0)
     p2.six()
     p3.six()
     lax.fori_loop(0, plain, dy_step, 0)
-    for ring in xb:
-        ring.four()
-    lax.fori_loop(plain, steps, dy_step, 0)
     cut(1, dy0)
     lax.fori_loop(0, strips, finish, 0)
     links.drain()

time: 180 us -> 181 us (level)
  Pallas kernels: 171 us -> 173 us
where the time goes in v4:
time: 181 us; the launch traced here: 178 us
  Pallas kernels  173 us (96%)
  local copies, waits for them, and re-layouts  2.93 us (2%)
    pallas_call x1, Pallas kernels, per_device(): pl.pallas_call(functools.partial(return_kernel, dims), name='grads_back',...  82.6 us
    pallas_call x1, Pallas kernels, per_device(): pl.pallas_call(functools.partial(dispatch_kernel, dims), name='dispatch',...  80.9 us
    pallas_call x1, Pallas kernels, per_device(): pl.pallas_call(functools.partial(combine_kernel, replicas), name='combine...  9.31 us

profile of v4, /device:TPU:1, one launch (start us, length us, event | category | flops | bytes accessed | tf_op | source)
XLA Modules:
  0.0 177.8 jit_solution(4009257931145161214)
XLA Ops:
  0.6 0.1 pad.2.clone
  0.7 0.7 convert_element_type.3
  1.4 0.1 copy.14
  1.5 0.8 copy.15
  2.3 0.7 maximum_maximum_fusion.meta
  2.9 80.9 %dispatch.1 = (bf16[384,768]{1,0:T(8,128)(2,1)}, bf16[384,128]{1,0:T(8,128)(2,1)}, bf16[2,1024,256]{2,1,0:T(8,128)(2,1)}, bf16[1024,128]{1,0:T(8,128)(2,1)}) custom-call(bf16[32,7168]{1,0:T(8,128)(2,1)} %tokens.1, bf16[32,7168]{1,0:T(8,128)(2,1)} %cotangent.1, bf16[32,128]{1,0:T(8,128)(2,1)} %maximum_maximum_fusion.meta, bf16[7168,256]{1,0:T(8,128)(2,1)} %bitcast.5, ...), custom_call_target="tpu_custom_call" | custom-call | tf_op jit(solution)/shard_map/dispatch/pallas_call | solution.py:885
  83.9 82.6 %grads_back.1 = (bf16[32,3,224,256]{3,2,1,0:T(8,128)(2,1)}, bf16[32,1792]{1,0:T(8,128)(2,1)}, bf16[32,128]{1,0:T(8,128)(2,1)}) custom-call(bf16[384,768]{1,0:T(8,128)(2,1)} %get-tuple-element.10.acts, bf16[384,128]{1,0:T(8,128)(2,1)} %get-tuple-element.11.score, bf16[1024,128]{1,0:T(8,128)(2,1)} %get-tuple-element.12.meta_all, ...), custom_call_target="tpu_custom_call" | custom-call | tf_op jit(solution)/shard_map/grads_back/pallas_call | solution.py:920
  166.5 1.3 copy.16
  167.8 0.0 copy-start
  167.8 9.3 %combine.1 = bf16[28,3,224,256]{3,2,1,0:T(8,128)(2,1)} custom-call(s32[4]{0:T(128)} %owners.1, bf16[32,3,224,256]{3,2,1,0:T(8,128)(2,1)} %get-tuple-element.16.slot_grads), custom_call_target="tpu_custom_call" | custom-call | tf_op jit(solution)/shard_map/combine/pallas_call | solution.py:962
  177.2 0.0 copy-done
  177.2 0.6 copy.18
  (1 shorter events, 0.0 us)
Async XLA Ops:
  167.8 9.3 %copy-start = (bf16[32,1792]{1,0:T(8,128)(2,1)S(1)}, bf16[32,1792]{1,0:T(8,128)(2,1)}, u32[]{:S(2)}) copy-start(bf16[32,1792]{1,0:T(8,128)(2,1)} %get-tuple-element.26) | copy-start | bytes 344068
